TPU v7x, 512 devices: a whole 4x8x8 slice. The times are simulated.
512 devices in a mesh: gx: 64 (over y_hi, z, core), gy: 8 (over x, y_lo).
Axes of the slice: x: 4, y: 8 (y_hi: 4, y_lo: 2; y = y_hi * 2 + y_lo), z: 8, core: 2. Of those that a mesh axis runs over, the one named last changes fastest.
Arguments:
- e_field: float32 [3, 16, 1024, 1024], P(None, None, 'gx', 'gy'), may hold values from -6 to 6
- h_field: float32 [3, 16, 1024, 1024], P(None, None, 'gx', 'gy'), may hold values from -6 to 6
- pole_now: float32 [2, 3, 16, 1024, 1024], P(None, None, None, 'gx', 'gy'), may hold values from -6 to 6
- pole_prev: float32 [2, 3, 16, 1024, 1024], P(None, None, None, 'gx', 'gy'), may hold values from -6 to 6
- material: int32 [16, 1024, 1024], P(None, 'gx', 'gy'), may hold values from 0 to 3, as said below
- eps_inf: float32 [4], replicated, may hold values from 1.5 to 6
- resonance: float32 [4, 2], replicated, may hold values from 0.3 to 1.6
- damping: float32 [4, 2], replicated, may hold values from 0.05 to 1
- strength: float32 [4, 2], replicated, may hold values from 0.5 to 3
Outputs:
- e_out: float32 [3, 16, 1024, 1024], P(None, None, 'gx', 'gy')
- h_out: float32 [3, 16, 1024, 1024], P(None, None, 'gx', 'gy')
Inputs may be any that keep to these rules, and one draw needn't show every extreme that they name: `material`: 0 perovskite, 1 ITO junction, 2 silicon, 3 air; along z each column runs air, perovskite, junction, silicon, each layer at least one cell thick, with interface depths varying from column to column.
All inputs are finite; a program needn't handle non-finite values.
Results may differ from a plain program's by a relative error of at most 0.0001.
Values sent between devices are 32-bit elements; how exact they have to be, the bound alone decides.
A program may use at most 128 MiB of HBM per device.

v0:
```python
import jax
import jax.numpy as jnp
from jax import lax
from jax.sharding import PartitionSpec as P

time_step = 0.5


def passed_along(block, axis, distance):
    devices = range(lax.axis_size(axis))
    route = [((i - distance) % len(devices), i) for i in devices]
    return lax.ppermute(block, axis, route)


def cell_values(material, table):
    total = jnp.zeros(table.shape[1:] + material.shape, jnp.float32)
    for index in range(table.shape[0]):
        entry = table[index].reshape(table.shape[1:] + (1,) * material.ndim)
        total = total + jnp.where(material[None] == index, entry, jnp.float32(0.0))
    return total


def coefficients(material, eps_inf, resonance, damping, strength):
    air = jnp.arange(eps_inf.shape[0]) == 3
    eps_tab = jnp.where(air, jnp.float32(1.0), eps_inf)
    str_tab = jnp.where(air[:, None], jnp.float32(0.0), strength)
    wdt = resonance * resonance * (time_step * time_step)
    denom = 1.0 + damping * (time_step / 2.0)
    one_tab = (2.0 - wdt) / denom
    two_tab = (damping * (time_step / 2.0) - 1.0) / denom
    three_tab = str_tab * wdt / denom
    inv_eps = 1.0 / cell_values(material, eps_tab[:, None])[0]
    return (
        cell_values(material, one_tab),
        cell_values(material, two_tab),
        cell_values(material, three_tab),
        inv_eps,
    )


def forward_z(field):
    return jnp.concatenate([field[1:], jnp.zeros_like(field[:1])], 0) - field


def backward_z(field):
    return field - jnp.concatenate([jnp.zeros_like(field[:1]), field[:-1]], 0)


def sectioned_fields(e_field, h_field):
    ex, ey, ez = (e_field[0], e_field[1], e_field[2])
    hx, hy, hz = (h_field[0], h_field[1], h_field[2])
    ahead_x = passed_along(e_field[1:3, :, 0:1, :], "gx", -1)
    ahead_y = passed_along(jnp.stack([ex[:, :, 0:1], ez[:, :, 0:1]]), "gy", -1)
    dx_ey = jnp.concatenate([ey[:, 1:], ahead_x[0]], 1) - ey
    dx_ez = jnp.concatenate([ez[:, 1:], ahead_x[1]], 1) - ez
    dy_ex = jnp.concatenate([ex[:, :, 1:], ahead_y[0]], 2) - ex
    dy_ez = jnp.concatenate([ez[:, :, 1:], ahead_y[1]], 2) - ez
    hx = hx - time_step * (dy_ez - forward_z(ey))
    hy = hy - time_step * (forward_z(ex) - dx_ez)
    hz = hz - time_step * (dx_ey - dy_ex)
    newer = jnp.stack([hx, hy, hz])
    behind_x = passed_along(newer[1:3, :, -1:, :], "gx", 1)
    behind_y = passed_along(jnp.stack([hx[:, :, -1:], hz[:, :, -1:]]), "gy", 1)
    bx_hy = hy - jnp.concatenate([behind_x[0], hy[:, :-1]], 1)
    bx_hz = hz - jnp.concatenate([behind_x[1], hz[:, :-1]], 1)
    by_hx = hx - jnp.concatenate([behind_y[0], hx[:, :, :-1]], 2)
    by_hz = hz - jnp.concatenate([behind_y[1], hz[:, :, :-1]], 2)
    curl = jnp.stack([by_hz - backward_z(hy), backward_z(hx) - bx_hz, bx_hy - by_hx])
    return (newer, curl)


def body(e_field, h_field, pole_now, pole_prev, material, eps_inf, resonance, damping, strength):
    coef_one, coef_two, coef_three, inv_eps = coefficients(
        material, eps_inf, resonance, damping, strength
    )
    for step in range(2):
        newer, curl = sectioned_fields(e_field, h_field)
        fresh = (
            coef_one[:, None] * pole_now
            + coef_two[:, None] * pole_prev
            + coef_three[:, None] * e_field[None]
        )
        change = jnp.sum(fresh - pole_now, axis=0)
        e_field = e_field + (time_step * curl - change) * inv_eps[None]
        h_field = newer
        pole_prev = pole_now
        pole_now = fresh
    return (e_field, h_field)


def solution(mesh):
    in_specs = (
        P(None, None, "gx", "gy"),
        P(None, None, "gx", "gy"),
        P(None, None, None, "gx", "gy"),
        P(None, None, None, "gx", "gy"),
        P(None, "gx", "gy"),
        P(),
        P(),
        P(),
        P(),
    )
    out_specs = (P(None, None, "gx", "gy"), P(None, None, "gx", "gy"))
    return jax.shard_map(body, mesh=mesh, in_specs=in_specs, out_specs=out_specs, check_vma=False)
```

profile of v0, /device:TPU:1, one launch (start us, length us, event | category | flops | bytes accessed | tf_op | source)
XLA Modules:
  0.0 76.7 jit_solution(5166533917237780493)
XLA Ops:
  0.6 0.9 %slice.255 = f32[2,16,1,128]{3,2,1,0:T(1,128)S(1)} slice(f32[3,16,16,128]{3,2,1,0:T(8,128)} %param.9), slice={[1:3], [0:16], [0:1], [0:128]} | slice | bytes 32768 | tf_op jit(solution)/shard_map/slice | solution.py:52
  1.6 8.9 %collective-permute-start = (f32[2,16,1,128]{3,1,2,0:T(8,128)S(1)}, f32[2,16,1,128]{3,1,2,0:T(8,128)S(1)}, u32[]{:S(2)}, u32[]{:S(2)}) collective-permute-start(f32[2,16,1,128]{3,1,2,0:T(8,128)S(1)} %bitcast.171), channel_id=1, source_target_pairs={{8,0},{16,8},{24,16},{32,24},{40,32},{48,40},{56,48},{64,56},{72,6... | collective-permute-start | bytes 49160 | tf_op jit(solution)/shard_map/ppermute | solution.py:12
  10.5 1.1 %slice_bitcast_fusion.4 = (f32[16,16,128]{2,1,0:T(8,128)S(1)}, f32[16,16,128]{2,1,0:T(8,128)S(1)}, f32[16,16,128]{2,1,0:T(8,128)S(1)}) fusion(f32[3,16,16,128]{3,2,1,0:T(8,128)} %param.9), kind=kLoop, calls=%fused_computation.84 | loop fusion | bytes 786432 | tf_op jit(solution)/shard_map/squeeze | solution.py:50
  11.7 1.9 %collective-permute-start.1 = (f32[2,16,16,1]{2,1,3,0:T(8,128)S(1)}, f32[2,16,16,1]{2,1,3,0:T(8,128)S(1)}, u32[]{:S(2)}, u32[]{:S(2)}) collective-permute-start(f32[2,16,16,1]{2,1,3,0:T(8,128)S(1)} %pad_maximum_fusion.3), channel_id=1, source_target_pairs={{1,0},{2,1},{3,2},{4,3},{5,4},{6,5},{7,6},{0,7},{9,8},{10,9},{11,1... | collective-permute-start | bytes 6152 | tf_op jit(solution)/shard_map/ppermute | solution.py:12
  13.7 0.7 slice_bitcast_fusion.9
  14.4 0.8 %fusion.44 = (f32[16,16,127]{2,1,0:T(8,128)}, f32[1,16,16,127]{3,2,1,0:T(8,128)}) fusion(f32[16,16,128]{2,1,0:T(8,128)S(1)} %get-tuple-element.40), kind=kLoop, calls=%fused_computation.133 | loop fusion | bytes 390144 | tf_op jit(solution)/shard_map/slice | solution.py:56
  15.2 0.7 fusion.50
  15.9 0.2 slice_reduce_fusion.19
  16.1 0.7 fusion.45
  16.9 0.3 slice_reduce_fusion.11
  17.2 3.3 %add_divide_fusion = (f32[16,16,128]{2,1,0:T(8,128)}, pred[16,16,128]{2,1,0:T(8,128)(4,1)S(1)}, pred[16,16,128]{2,1,0:T(8,128)(4,1)S(1)}, pred[16,16,128]{2,1,0:T(8,128)(4,1)S(1)}, pred[16,16,128]{2,1,0:T(8,128)(4,1)S(1)}) fusion(f32[]{:T(128)} %bitcast.30, f32[]{:T(128)} %bitcast.29, f32[]{:T(128)} %bitcast.28, f32[]{:T(128)} %bitcast.27, ...), kind=kLoop, calls=%fused_computation.80 | loop fusion | flops 393216 | bytes 393232 | tf_op jit(solution)/shard_map/div | solution.py:32
  20.5 0.3 select_add_fusion.2
  20.8 1.0 %subtract_reduce_fusion.1 = f32[3,16,16,128]{3,2,1,0:T(8,128)} fusion(f32[2,3,16,16,128]{4,3,2,1,0:T(8,128)S(1)} %copy-done.1, f32[2,3,16,16,128]{4,3,2,1,0:T(8,128)S(1)} %copy-done.2, f32[3,16,16,128]{3,2,1,0:T(8,128)S(1)} %copy-done, f32[2,16,16,128]{3,2,1,0:T(8,128)S(1)} %get-tuple-element.58, f32[2,16,16,128]{3,2,1,0:T(8,128)S(1)} %get-tuple-element.59, ...), kind=kLoop, calls=%fused_computation.1 | loop fusion | flops 1277952 | bytes 3145728 | tf_op jit(solution)/shard_map/reduce_sum | solution.py:83
  21.7 0.6 slice.345
  22.4 0.8 slice.339
  23.2 0.8 %copy.252 = f32[16,16,1]{2,1,0:T(8,128)} copy(f32[16,16,1]{1,0,2:T(8,128)S(1)} %get-tuple-element.73) | data formatting | bytes 2048 | tf_op jit(solution)/shard_map/squeeze | solution.py:56
  24.0 0.8 %copy.253 = f32[16,16,1]{2,1,0:T(8,128)} copy(f32[16,16,1]{1,0,2:T(8,128)S(1)} %get-tuple-element.74) | data formatting | bytes 2048 | tf_op jit(solution)/shard_map/squeeze | solution.py:57
  24.8 0.8 %copy.257 = f32[1,16,16,1]{3,2,1,0:T(8,128)} copy(f32[1,16,16,1]{2,1,3,0:T(8,128)S(1)} %get-tuple-element.75) | data formatting | bytes 2048 | tf_op jit(solution)/shard_map/slice | solution.py:56
  25.6 1.5 %fusion.8 = (f32[16,16,128]{2,1,0:T(8,128)S(1)}, f32[16,16,128]{2,1,0:T(8,128)S(1)}, f32[16,16,128]{2,1,0:T(8,128)S(1)}) fusion(f32[16,1,128]{2,1,0:T(1,128)S(1)} %bitcast.151, f32[16,15,128]{2,1,0:T(8,128)} %get-tuple-element.55, f32[16,16,1]{2,1,0:T(8,128)} %copy.252, f32[16,16,127]{2,1,0:T(8,128)} %get-tuple-element.53, ...), kind=kLoop, calls=%fused_computation.27 | loop fusion | flops 622592 | bytes 1949696 | tf_op jit(solution)/shard_map/sub | solution.py:60
  27.2 0.2 slice_reduce_fusion.4
  27.4 0.2 slice_reduce_fusion.5
  27.6 3.4 %collective-permute-start.2 = (f32[2,16,16,1]{2,1,3,0:T(8,128)S(1)}, f32[2,16,16,1]{2,1,3,0:T(8,128)S(1)}, u32[]{:S(2)}, u32[]{:S(2)}) collective-permute-start(f32[2,16,16,1]{2,1,3,0:T(8,128)S(1)} %pad_maximum_fusion.4), channel_id=1, source_target_pairs={{7,0},{0,1},{1,2},{2,3},{3,4},{4,5},{5,6},{6,7},{15,8},{8,9},{9,10... | collective-permute-start | bytes 6152 | tf_op jit(solution)/shard_map/ppermute | solution.py:12
  31.0 1.0 %fusion.19 = f32[1,16,16,128]{3,2,1,0:T(8,128)S(1)} fusion(f32[1,16,1,128]{3,2,1,0:T(1,128)S(1)} %bitcast.152, f32[1,16,15,128]{3,2,1,0:T(8,128)S(1)} %copy-done.11, f32[1,16,16,1]{3,2,1,0:T(8,128)S(1)} %copy-done.12, f32[1,16,16,127]{3,2,1,0:T(8,128)S(1)} %copy-done.10, f32[3,16,16,128]{3,2,1,0:T(8,128)S(1)} %copy-done, f32[3,16,16,128]{3,2,1,0:T(8,128)} %param.10), kind=kLoop, calls=%fused_computation.43 | loop fusion | flops 229376 | bytes 786432 | tf_op jit(solution)/shard_map/sub | solution.py:60
  32.0 0.6 copy-done.5
  32.6 0.7 slice.347
  33.3 0.7 slice.348
  34.0 1.9 %collective-permute-start.3 = (f32[2,16,1,128]{3,1,2,0:T(8,128)S(1)}, f32[2,16,1,128]{3,1,2,0:T(8,128)}, u32[]{:S(2)}, u32[]{:S(2)}) collective-permute-start(f32[2,16,1,128]{3,1,2,0:T(8,128)S(1)} %bitcast.170), channel_id=1, source_target_pairs={{504,0},{0,8},{8,16},{16,24},{24,32},{32,40},{40,48},{48,56},{56,6... | collective-permute-start | bytes 49160 | tf_op jit(solution)/shard_map/ppermute | solution.py:12
  35.9 0.2 copy.254
  36.2 8.6 %collective-permute-done.3 = f32[2,16,1,128]{3,1,2,0:T(8,128)} collective-permute-done((f32[2,16,1,128]{3,1,2,0:T(8,128)S(1)}, f32[2,16,1,128]{3,1,2,0:T(8,128)}, u32[]{:S(2)}, u32[]{:S(2)}) %collective-permute-start.3) | collective-permute-done | bytes 16416 | tf_op jit(solution)/shard_map/ppermute | solution.py:12
  44.9 0.7 fusion.48
  45.6 1.1 %fusion.13 = (f32[1,16,16,128]{3,2,1,0:T(8,128)S(1)}, f32[1,16,16,128]{3,2,1,0:T(8,128)S(1)}, f32[1,16,16,128]{3,2,1,0:T(8,128)S(1)}) fusion(f32[16,16,128]{2,1,0:T(8,128)S(1)} %get-tuple-element.27, f32[16,16,127]{2,1,0:T(8,128)S(1)} %bitcast.139, f32[16,16,1]{2,1,0:T(8,128)S(1)} %copy.254, f32[16,16,128]{2,1,0:T(8,128)S(1)} %get-tuple-element.28, ...), kind=kLoop, calls=%fused_computation.35 | loop fusion | flops 425984 | bytes 1556480 | tf_op jit(solution)/shard_map/stack | solution.py:68
  46.8 1.1 %subtract_reduce_fusion = f32[3,16,16,128]{3,2,1,0:T(8,128)} fusion(f32[2,3,16,16,128]{4,3,2,1,0:T(8,128)S(1)} %copy-done.1, f32[2,3,16,16,128]{4,3,2,1,0:T(8,128)S(1)} %copy-done.2, f32[3,16,16,128]{3,2,1,0:T(8,128)S(1)} %fusion.2, f32[3,16,16,128]{3,2,1,0:T(8,128)S(1)} %copy-done, f32[2,16,16,128]{3,2,1,0:T(8,128)S(1)} %get-tuple-element.58, ...), kind=kLoop, calls=%fused_computation | loop fusion | flops 2260992 | bytes 3538944 | tf_op jit(solution)/shard_map/reduce_sum | solution.py:83
  48.5 8.6 %collective-permute-start.4 = (f32[2,16,1,128]{3,1,2,0:T(8,128)S(1)}, f32[2,16,1,128]{3,1,2,0:T(8,128)S(1)}, u32[]{:S(2)}, u32[]{:S(2)}) collective-permute-start(f32[2,16,1,128]{3,1,2,0:T(8,128)S(1)} %bitcast.172), channel_id=1, source_target_pairs={{8,0},{16,8},{24,16},{32,24},{40,32},{48,40},{56,48},{64,56},{72,6... | collective-permute-start | bytes 49160 | tf_op jit(solution)/shard_map/ppermute | solution.py:12
  57.1 5.8 %collective-permute-start.5 = (f32[2,16,16,1]{2,1,3,0:T(8,128)S(1)}, f32[2,16,16,1]{2,1,3,0:T(8,128)S(1)}, u32[]{:S(2)}, u32[]{:S(2)}) collective-permute-start(f32[2,16,16,1]{2,1,3,0:T(8,128)S(1)} %pad_maximum_fusion.5), channel_id=1, source_target_pairs={{1,0},{2,1},{3,2},{4,3},{5,4},{6,5},{7,6},{0,7},{9,8},{10,9},{11,1... | collective-permute-start | bytes 6152 | tf_op jit(solution)/shard_map/ppermute | solution.py:12
  62.8 0.8 %collective-permute-done.5 = f32[2,16,16,1]{2,1,3,0:T(8,128)S(1)} collective-permute-done((f32[2,16,16,1]{2,1,3,0:T(8,128)S(1)}, f32[2,16,16,1]{2,1,3,0:T(8,128)S(1)}, u32[]{:S(2)}, u32[]{:S(2)}) %collective-permute-start.5) | collective-permute-done | bytes 2080 | tf_op jit(solution)/shard_map/ppermute | solution.py:12
  63.7 0.2 copy.264
  64.2 0.2 fusion.26
  64.4 0.2 slice_reduce_fusion
  64.6 0.2 slice_reduce_fusion.1
  64.8 0.5 copy-done.6
  65.4 1.9 %collective-permute-start.7 = (f32[2,16,1,128]{3,1,2,0:T(8,128)S(1)}, f32[2,16,1,128]{3,1,2,0:T(8,128)S(1)}, u32[]{:S(2)}, u32[]{:S(2)}) collective-permute-start(f32[2,16,1,128]{3,1,2,0:T(8,128)S(1)} %bitcast.169), channel_id=1, source_target_pairs={{504,0},{0,8},{8,16},{16,24},{24,32},{32,40},{40,48},{48,56},{56,6... | collective-permute-start | bytes 49160 | tf_op jit(solution)/shard_map/ppermute | solution.py:12
  67.4 1.9 %collective-permute-start.6 = (f32[2,16,16,1]{2,1,3,0:T(8,128)S(1)}, f32[2,16,16,1]{2,1,3,0:T(8,128)S(1)}, u32[]{:S(2)}, u32[]{:S(2)}) collective-permute-start(f32[2,16,16,1]{2,1,3,0:T(8,128)S(1)} %pad_maximum_fusion.6), channel_id=1, source_target_pairs={{7,0},{0,1},{1,2},{2,3},{3,4},{4,5},{5,6},{6,7},{15,8},{8,9},{9,10... | collective-permute-start | bytes 6152 | tf_op jit(solution)/shard_map/ppermute | solution.py:12
  69.3 0.8 %pad_maximum_fusion = f32[3,16,16,128]{3,2,1,0:T(8,128)} fusion(f32[1,16,16,128]{3,2,1,0:T(8,128)S(1)} %fusion.37, f32[1,16,16,128]{3,2,1,0:T(8,128)S(1)} %bitcast.145, f32[1,16,16,128]{3,2,1,0:T(8,128)S(1)} %bitcast.147), kind=kLoop, calls=%fused_computation.11 | loop fusion | flops 196608 | bytes 786432 | tf_op jit(solution)/shard_map/stack | solution.py:61
  70.1 4.4 %collective-permute-done.6 = f32[2,16,16,1]{2,1,3,0:T(8,128)S(1)} collective-permute-done((f32[2,16,16,1]{2,1,3,0:T(8,128)S(1)}, f32[2,16,16,1]{2,1,3,0:T(8,128)S(1)}, u32[]{:S(2)}, u32[]{:S(2)}) %collective-permute-start.6) | collective-permute-done | bytes 2080 | tf_op jit(solution)/shard_map/ppermute | solution.py:12
  74.5 0.2 copy.266
  74.9 0.2 fusion.31
  75.1 0.8 %copy-done.3 = f32[3,16,16,128]{3,2,1,0:T(8,128)S(1)} copy-done((f32[3,16,16,128]{3,2,1,0:T(8,128)S(1)}, f32[3,16,16,128]{3,2,1,0:T(8,128)}, u32[]{:S(2)}) %copy-start.3) | copy-done | bytes 393240
  75.9 0.8 %fusion.5 = f32[3,16,16,128]{3,2,1,0:T(8,128)} fusion(f32[3,16,16,128]{3,2,1,0:T(8,128)S(1)} %fusion.2, f32[3,16,16,128]{3,2,1,0:T(8,128)S(1)} %copy-done.3, f32[1,16,16,128]{3,2,1,0:T(8,128)S(1)} %get-tuple-element.44, f32[1,16,16,128]{3,2,1,0:T(8,128)S(1)} %get-tuple-element.45, f32[1,16,16,128]{3,2,1,0:T(8,128)S(1)} %get-tuple-element.43, ...), kind=kLoop, calls=%fused_computation.10 | loop fusion | flops 589824 | bytes 1703936 | tf_op jit(solution)/shard_map/add | solution.py:84
  (74 shorter events, 1.7 us)
Async XLA Ops:
  1.5 12.1 %copy-start = (f32[3,16,16,128]{3,2,1,0:T(8,128)S(1)}, f32[3,16,16,128]{3,2,1,0:T(8,128)}, u32[]{:S(2)}) copy-start(f32[3,16,16,128]{3,2,1,0:T(8,128)} %param.9) | copy-start | bytes 1179652
  1.6 24.1 %collective-permute-start = (f32[2,16,1,128]{3,1,2,0:T(8,128)S(1)}, f32[2,16,1,128]{3,1,2,0:T(8,128)S(1)}, u32[]{:S(2)}, u32[]{:S(2)}) collective-permute-start(f32[2,16,1,128]{3,1,2,0:T(8,128)S(1)} %bitcast.171), channel_id=1, source_target_pairs={{8,0},{16,8},{24,16},{32,24},{40,32},{48,40},{56,48},{64,56},{72,6... | collective-permute-start | bytes 49160 | tf_op jit(solution)/shard_map/ppermute | solution.py:12
  11.7 11.4 %collective-permute-start.1 = (f32[2,16,16,1]{2,1,3,0:T(8,128)S(1)}, f32[2,16,16,1]{2,1,3,0:T(8,128)S(1)}, u32[]{:S(2)}, u32[]{:S(2)}) collective-permute-start(f32[2,16,16,1]{2,1,3,0:T(8,128)S(1)} %pad_maximum_fusion.3), channel_id=1, source_target_pairs={{1,0},{2,1},{3,2},{4,3},{5,4},{6,5},{7,6},{0,7},{9,8},{10,9},{11,1... | collective-permute-start | bytes 6152 | tf_op jit(solution)/shard_map/ppermute | solution.py:12
  14.4 0.8 %copy-start.18 = (f32[4]{0:T(128)S(1)}, f32[4]{0:T(128)}, u32[]{:S(2)}) copy-start(f32[4]{0:T(128)} %param.14) | copy-start | bytes 52
  14.4 2.8 %copy-start.14 = (s32[16,16,128]{2,1,0:T(8,128)S(1)}, s32[16,16,128]{2,1,0:T(8,128)}, u32[]{:S(2)}) copy-start(s32[16,16,128]{2,1,0:T(8,128)} %param.13) | copy-start | bytes 393220
  15.2 0.7 copy-start.15
  15.2 0.7 copy-start.16
  15.2 0.7 copy-start.17
  16.1 4.6 %copy-start.2 = (f32[2,3,16,16,128]{4,3,2,1,0:T(8,128)S(1)}, f32[2,3,16,16,128]{4,3,2,1,0:T(8,128)}, u32[]{:S(2)}) copy-start(f32[2,3,16,16,128]{4,3,2,1,0:T(8,128)} %param.12) | copy-start | bytes 2359300
  16.9 3.9 %copy-start.1 = (f32[2,3,16,16,128]{4,3,2,1,0:T(8,128)S(1)}, f32[2,3,16,16,128]{4,3,2,1,0:T(8,128)}, u32[]{:S(2)}) copy-start(f32[2,3,16,16,128]{4,3,2,1,0:T(8,128)} %param.11) | copy-start | bytes 2359300
  23.2 2.5 %copy-start.9 = (f32[3,16,16,128]{3,2,1,0:T(8,128)S(1)}, f32[3,16,16,128]{3,2,1,0:T(8,128)}, u32[]{:S(2)}) copy-start(f32[3,16,16,128]{3,2,1,0:T(8,128)} %param.10) | copy-start | bytes 1179652
  25.6 5.3 %copy-start.12 = (f32[1,16,16,1]{3,2,1,0:T(8,128)S(1)}, f32[1,16,16,1]{3,2,1,0:T(8,128)}, u32[]{:S(2)}) copy-start(f32[1,16,16,1]{3,2,1,0:T(8,128)} %copy.257) | copy-start | bytes 3076
  27.1 3.8 %copy-start.10 = (f32[1,16,16,127]{3,2,1,0:T(8,128)S(1)}, f32[1,16,16,127]{3,2,1,0:T(8,128)}, u32[]{:S(2)}) copy-start(f32[1,16,16,127]{3,2,1,0:T(8,128)} %get-tuple-element.54) | copy-start | bytes 390148
  27.1 3.8 %copy-start.11 = (f32[1,16,15,128]{3,2,1,0:T(8,128)S(1)}, f32[1,16,15,128]{3,2,1,0:T(8,128)}, u32[]{:S(2)}) copy-start(f32[1,16,15,128]{3,2,1,0:T(8,128)} %get-tuple-element.56) | copy-start | bytes 368644
  27.6 8.3 %collective-permute-start.2 = (f32[2,16,16,1]{2,1,3,0:T(8,128)S(1)}, f32[2,16,16,1]{2,1,3,0:T(8,128)S(1)}, u32[]{:S(2)}, u32[]{:S(2)}) collective-permute-start(f32[2,16,16,1]{2,1,3,0:T(8,128)S(1)} %pad_maximum_fusion.4), channel_id=1, source_target_pairs={{7,0},{0,1},{1,2},{2,3},{3,4},{4,5},{5,6},{6,7},{15,8},{8,9},{9,10... | collective-permute-start | bytes 6152 | tf_op jit(solution)/shard_map/ppermute | solution.py:12
  32.0 0.7 copy-start.5
  34.0 10.9 %collective-permute-start.3 = (f32[2,16,1,128]{3,1,2,0:T(8,128)S(1)}, f32[2,16,1,128]{3,1,2,0:T(8,128)}, u32[]{:S(2)}, u32[]{:S(2)}) collective-permute-start(f32[2,16,1,128]{3,1,2,0:T(8,128)S(1)} %bitcast.170), channel_id=1, source_target_pairs={{504,0},{0,8},{8,16},{16,24},{24,32},{32,40},{40,48},{48,56},{56,6... | collective-permute-start | bytes 49160 | tf_op jit(solution)/shard_map/ppermute | solution.py:12
  36.1 9.5 %copy-start.13 = (f32[15,16,128]{2,1,0:T(8,128)S(1)}, f32[15,16,128]{2,1,0:T(8,128)}, u32[]{:S(2)}) copy-start(f32[15,16,128]{2,1,0:T(8,128)} %slice.347) | copy-start | bytes 368644
  45.6 1.1 %copy-start.4 = (f32[3,16,16,128]{3,2,1,0:T(8,128)S(1)}, f32[3,16,16,128]{3,2,1,0:T(8,128)}, u32[]{:S(2)}) copy-start(f32[3,16,16,128]{3,2,1,0:T(8,128)} %subtract_reduce_fusion.1) | copy-start | bytes 1179652
  45.6 1.1 %copy-start.7 = (f32[16,16,128]{2,1,0:T(8,128)S(1)}, f32[16,16,128]{2,1,0:T(8,128)}, u32[]{:S(2)}) copy-start(f32[16,16,128]{2,1,0:T(8,128)} %get-tuple-element.22) | copy-start | bytes 393220
  48.5 15.7 %collective-permute-start.4 = (f32[2,16,1,128]{3,1,2,0:T(8,128)S(1)}, f32[2,16,1,128]{3,1,2,0:T(8,128)S(1)}, u32[]{:S(2)}, u32[]{:S(2)}) collective-permute-start(f32[2,16,1,128]{3,1,2,0:T(8,128)S(1)} %bitcast.172), channel_id=1, source_target_pairs={{8,0},{16,8},{24,16},{32,24},{40,32},{48,40},{56,48},{64,56},{72,6... | collective-permute-start | bytes 49160 | tf_op jit(solution)/shard_map/ppermute | solution.py:12
  57.1 6.6 %collective-permute-start.5 = (f32[2,16,16,1]{2,1,3,0:T(8,128)S(1)}, f32[2,16,16,1]{2,1,3,0:T(8,128)S(1)}, u32[]{:S(2)}, u32[]{:S(2)}) collective-permute-start(f32[2,16,16,1]{2,1,3,0:T(8,128)S(1)} %pad_maximum_fusion.5), channel_id=1, source_target_pairs={{1,0},{2,1},{3,2},{4,3},{5,4},{6,5},{7,6},{0,7},{9,8},{10,9},{11,1... | collective-permute-start | bytes 6152 | tf_op jit(solution)/shard_map/ppermute | solution.py:12
  64.4 0.9 %copy-start.6 = (f32[1,16,16,128]{3,2,1,0:T(8,128)S(1)}, f32[1,16,16,128]{3,2,1,0:T(8,128)}, u32[]{:S(2)}) copy-start(f32[1,16,16,128]{3,2,1,0:T(8,128)} %copy-done.5) | copy-start | bytes 393220
  65.4 9.4 %collective-permute-start.7 = (f32[2,16,1,128]{3,1,2,0:T(8,128)S(1)}, f32[2,16,1,128]{3,1,2,0:T(8,128)S(1)}, u32[]{:S(2)}, u32[]{:S(2)}) collective-permute-start(f32[2,16,1,128]{3,1,2,0:T(8,128)S(1)} %bitcast.169), channel_id=1, source_target_pairs={{504,0},{0,8},{8,16},{16,24},{24,32},{32,40},{40,48},{48,56},{56,6... | collective-permute-start | bytes 49160 | tf_op jit(solution)/shard_map/ppermute | solution.py:12
  67.4 7.2 %collective-permute-start.6 = (f32[2,16,16,1]{2,1,3,0:T(8,128)S(1)}, f32[2,16,16,1]{2,1,3,0:T(8,128)S(1)}, u32[]{:S(2)}, u32[]{:S(2)}) collective-permute-start(f32[2,16,16,1]{2,1,3,0:T(8,128)S(1)} %pad_maximum_fusion.6), channel_id=1, source_target_pairs={{7,0},{0,1},{1,2},{2,3},{3,4},{4,5},{5,6},{6,7},{15,8},{8,9},{9,10... | collective-permute-start | bytes 6152 | tf_op jit(solution)/shard_map/ppermute | solution.py:12
  74.9 1.0 %copy-start.3 = (f32[3,16,16,128]{3,2,1,0:T(8,128)S(1)}, f32[3,16,16,128]{3,2,1,0:T(8,128)}, u32[]{:S(2)}) copy-start(f32[3,16,16,128]{3,2,1,0:T(8,128)} %subtract_reduce_fusion) | copy-start | bytes 1179652
  74.9 1.0 %copy-start.8 = (f32[16,16,128]{2,1,0:T(8,128)S(1)}, f32[16,16,128]{2,1,0:T(8,128)}, u32[]{:S(2)}) copy-start(f32[16,16,128]{2,1,0:T(8,128)} %get-tuple-element.22) | copy-start | bytes 393220
where the time goes:
time: 77.3 us; the launch traced here: 76.7 us
  starting transfers between devices  34.3 us (44%)
  local copies, waits for them, and re-layouts  15.9 us (21%)
  waiting for transfers between devices  13.9 us (18%)
  other arithmetic  11.5 us (15%)
  between operations  1.13 us (1%)
    ppermute x8, starting transfers between devices, passed_along(): return lax.ppermute(block, axis, route)  34.3 us
    ppermute x8, waiting for transfers between devices, passed_along(): return lax.ppermute(block, axis, route)  13.9 us
    div x1, other arithmetic, coefficients(): inv_eps = 1.0 / cell_values(material, eps_tab[:, None])[0]  3.29 us
    sub x4, other arithmetic, sectioned_fields(): hz = hz - time_step * (dx_ey - dy_ex)  2.81 us
    reduce_sum x2, other arithmetic, body(): change = jnp.sum(fresh - pole_now, axis=0)  2.08 us
    unnamed x38, local copies, waits for them, and re-layouts  2.02 us
    slice x4, local copies, waits for them, and re-layouts, sectioned_fields(): dy_ex = jnp.concatenate([ex[:, :, 1:], ahead_y[0]], 2) - ex  1.89 us
  transfers between devices with their start and end apart: 8, of which 3 were waited for; matrix products, arithmetic and copies ran while one was open for 23% of the time, Pallas kernels for 0%

commit v1 on v0

v1 whole, which is shorter than its diff:
```python
import jax
import jax.numpy as jnp
from jax import lax
from jax.experimental import pallas as pl
from jax.experimental.pallas import tpu as pltpu
from jax.sharding import PartitionSpec as P

MESH = pl.DeviceIdType.MESH
DT = 0.5
NZ = 16
ROWS = 16
LANES = 128
TOP = 8
END = TOP + ROWS
TILE = (8, LANES)


def fill_tables(tables, eps_ref, res_ref, damp_ref, str_ref):
    for m in range(4):
        one = jnp.ones(TILE, jnp.float32)
        inv = one if m == 3 else one / jnp.full(TILE, eps_ref[m])
        c3_sum = jnp.zeros(TILE, jnp.float32)
        r = jnp.zeros(TILE, jnp.float32)
        for k in range(2):
            res = jnp.full(TILE, res_ref[m, k])
            damp = jnp.full(TILE, damp_ref[m, k])
            gain = jnp.full(TILE, str_ref[m, k])
            if m == 3:
                gain = jnp.zeros(TILE, jnp.float32)
            w = res * res * (DT * DT)
            s = 1.0 + damp * (DT / 2.0)
            c1 = (2.0 - w) / s
            c2 = (damp * (DT / 2.0) - 1.0) / s
            c3 = gain * w / s
            g = inv * (1.0 - c1)
            h = -inv * c2
            tables[2 + k, m] = g
            tables[4 + k, m] = h
            tables[6 + k, m] = g * c1 + h
            tables[8 + k, m] = g * c2
            c3_sum = c3_sum + c3
            r = r + g * c3
        tables[0, m] = 1.0 - inv * c3_sum
        tables[1, m] = inv * DT
        tables[10, m] = r


def kernel(
    e_hbm, h_hbm, now_hbm, prev_hbm, mat_hbm, eps_ref, res_ref, damp_ref, str_ref,
    e_out, h_out,
    eh, ad, now, prev, mat, tables, keep, late, h1, e1, h2, e2, strips, wide, sh1, se1, sh2,
    load_sem, send_sem, recv_sem, out_sem,
):
    gx, gy = lax.axis_index("gx"), lax.axis_index("gy")
    nx, ny = lax.axis_size("gx"), lax.axis_size("gy")
    xp, xn = lax.rem(gx + nx - 1, nx), lax.rem(gx + 1, nx)
    yp, yn = lax.rem(gy + ny - 1, ny), lax.rem(gy + 1, ny)

    loads = [
        pltpu.make_async_copy(e_hbm, eh.at[0:3, 1 : NZ + 1, TOP:END, :], load_sem.at[0]),
        pltpu.make_async_copy(h_hbm, eh.at[3:6, 1 : NZ + 1, TOP:END, :], load_sem.at[1]),
        pltpu.make_async_copy(mat_hbm, mat, load_sem.at[2]),
        pltpu.make_async_copy(now_hbm, now, load_sem.at[3]),
        pltpu.make_async_copy(prev_hbm, prev, load_sem.at[4]),
    ]
    barrier = pltpu.get_barrier_semaphore()
    for d in ((xp, gy), (xn, gy), (gx, yp), (gx, yn), (xp, yp), (xp, yn), (xn, yp), (xn, yn)):
        pl.semaphore_signal(barrier, inc=1, device_id=d, device_id_type=MESH)
    for c in loads:
        c.start()
    fill_tables(tables, eps_ref, res_ref, damp_ref, str_ref)
    zero = jnp.zeros((40, LANES), jnp.float32)
    for c in range(3):
        eh[c, NZ + 1] = zero
        e1[c, NZ] = zero
        h1[c, 0] = zero
        h2[c, 0] = zero
    pl.semaphore_wait(barrier, 8)

    def send(index, src, dst, device):
        c = pltpu.make_async_remote_copy(
            src_ref=src, dst_ref=dst, send_sem=send_sem.at[index], recv_sem=recv_sem.at[index],
            device_id=device, device_id_type=MESH,
        )
        c.start()
        return c

    inside = pl.ds(1, NZ)
    sends = [
        send(0, e_hbm.at[:, :, 14:16, :], eh.at[0:3, inside, 6:8, :], (xn, gy)),
        send(1, h_hbm.at[:, :, 14:16, :], eh.at[3:6, inside, 6:8, :], (xn, gy)),
        send(2, e_hbm.at[:, :, 0:2, :], eh.at[0:3, inside, 24:26, :], (xp, gy)),
        send(3, h_hbm.at[:, :, 0:1, :], eh.at[3:6, inside, 24:25, :], (xp, gy)),
    ]
    for c in loads:
        c.wait()

    def local(z, _):
        for b in (0, 8):
            kind = mat[z, b : b + 8, :]
            low = (kind & 1) == 1
            high = kind >= 2

            def value(i):
                return jnp.where(
                    high,
                    jnp.where(low, tables[i, 3], tables[i, 2]),
                    jnp.where(low, tables[i, 1], tables[i, 0]),
                )

            e, d, g0, g1, w0, w1, p0, p1, q0, q1, r = [value(i) for i in range(11)]
            rows = slice(TOP + b, TOP + b + 8)
            keep[z, b : b + 8, :] = e
            ad[3, z, rows, :] = d
            for c in range(3):
                f = eh[c, z + 1, rows, :]
                n0, n1 = now[0, c, z, b : b + 8, :], now[1, c, z, b : b + 8, :]
                m0, m1 = prev[0, c, z, b : b + 8, :], prev[1, c, z, b : b + 8, :]
                ad[c, z, rows, :] = (e * f + (g0 * n0 + g1 * n1)) + (w0 * m0 + w1 * m1)
                late[c, z, b : b + 8, :] = (r * f + (p0 * n0 + p1 * n1)) + (q0 * m0 + q1 * m1)
        return 0

    lax.fori_loop(0, NZ, local, 0)

    lane = lax.broadcasted_iota(jnp.int32, TILE, 1)
    group = lane // 8
    slot = lane % 8

    def pack(z, held):
        mine = group == z
        out = []
        for i in range(10):
            for b in (0, 8):
                rows = slice(TOP + b, TOP + b + 8)
                f = eh[i, z + 1, rows, :] if i < 6 else ad[i - 6, z, rows, :]
                out.append(jnp.where(mine, pltpu.roll(f, 8 * z + 2, 1), held[len(out)]))
        return tuple(out)

    held = lax.fori_loop(0, NZ, pack, tuple(jnp.zeros(TILE, jnp.float32) for _ in range(20)))
    for i in range(10):
        for j in range(2):
            strips[0, i, TOP + 8 * j : TOP + 8 * j + 8, :] = held[2 * i + j]

    own = strips.at[0]
    sends += [
        send(4, own.at[:, TOP:END, :], strips.at[1, :, TOP:END, :], (gx, yn)),
        send(5, own.at[:, TOP:END, :], strips.at[2, :, TOP:END, :], (gx, yp)),
        send(6, ad.at[:, :, 23:24, :], ad.at[:, :, 7:8, :], (xn, gy)),
        send(7, ad.at[:, :, 8:9, :], ad.at[:, :, 24:25, :], (xp, gy)),
        send(8, own.at[:, 22:24, :], strips.at[0, :, 6:8, :], (xn, gy)),
        send(9, own.at[:, 8:10, :], strips.at[0, :, 24:26, :], (xp, gy)),
        send(10, own.at[:, 22:24, :], strips.at[1, :, 6:8, :], (xn, yn)),
        send(11, own.at[:, 22:24, :], strips.at[2, :, 6:8, :], (xn, yp)),
        send(12, own.at[:, 8:10, :], strips.at[1, :, 24:26, :], (xp, yn)),
        send(13, own.at[:, 8:10, :], strips.at[2, :, 24:26, :], (xp, yp)),
    ]
    for c in sends:
        c.wait_recv()

    for i in range(10):
        for r in (6, 14, 22):
            rows = slice(r, r + 8)
            me, before, after = strips[0, i, rows, :], strips[1, i, rows, :], strips[2, i, rows, :]
            wide[i, rows, :] = jnp.where(
                slot < 4,
                jnp.where(slot < 2, me, after),
                pltpu.roll(jnp.where(slot < 2, before, me), 4, 1),
            )

    def ahead_z(f):
        return jnp.where(lane < 120, pltpu.roll(f, 120, 1), 0.0)

    def behind_z(f):
        return jnp.where(lane >= 8, pltpu.roll(f, 8, 1), 0.0)

    def h_step(ex, ey, ez, hx, hy, hz, ex_y, ez_y, ey_x, ez_x, ex_z, ey_z):
        return (
            hx - DT * ((ez_y - ez) - (ey_z - ey)),
            hy - DT * ((ex_z - ex) - (ez_x - ez)),
            hz - DT * ((ey_x - ey) - (ex_y - ex)),
        )

    def curl(hx, hy, hz, hx_y, hz_y, hy_x, hz_x, hx_z, hy_z):
        return (
            (hz - hz_y) - (hy - hy_z),
            (hx - hx_z) - (hz - hz_x),
            (hy - hy_x) - (hx - hx_y),
        )

    def strip_h(e_ref, h_ref, base, out, starts):
        for r in starts:
            rows, next_rows = slice(r, r + 8), slice(r + 1, r + 9)
            ex, ey, ez = (e_ref[i, rows, :] for i in range(3))
            new = h_step(
                ex, ey, ez, *(h_ref[base + i, rows, :] for i in range(3)),
                pltpu.roll(ex, 127, 1), pltpu.roll(ez, 127, 1),
                e_ref[1, next_rows, :], e_ref[2, next_rows, :], ahead_z(ex), ahead_z(ey),
            )
            for i in range(3):
                out[i, rows, :] = new[i]

    strip_h(wide, wide, 3, sh1, (6, 14, 22))
    for r in (7, 15, 23):
        rows, back_rows = slice(r, r + 8), slice(r - 1, r + 7)
        hx, hy, hz = (sh1[i, rows, :] for i in range(3))
        turn = curl(
            hx, hy, hz, pltpu.roll(hx, 1, 1), pltpu.roll(hz, 1, 1),
            sh1[1, back_rows, :], sh1[2, back_rows, :], behind_z(hx), behind_z(hy),
        )
        d = wide[9, rows, :]
        for i in range(3):
            se1[i, rows, :] = wide[6 + i, rows, :] + d * turn[i]
    strip_h(se1, sh1, 0, sh2, (7, 15, 23))

    def main_h(e_ref, shift, h_ref, h_base, strip, out, starts):
        def body(z, _):
            far = 125 - 8 * z
            for r in starts:
                rows, next_rows = slice(r, r + 8), slice(r + 1, r + 9)
                ex, ey, ez = (e_ref[i, z + shift, rows, :] for i in range(3))
                new = h_step(
                    ex, ey, ez, *(h_ref[h_base + i, z + 1, rows, :] for i in range(3)),
                    jnp.where(lane == 127, pltpu.roll(strip[0, rows, :], far, 1), pltpu.roll(ex, 127, 1)),
                    jnp.where(lane == 127, pltpu.roll(strip[2, rows, :], far, 1), pltpu.roll(ez, 127, 1)),
                    e_ref[1, z + shift, next_rows, :], e_ref[2, z + shift, next_rows, :],
                    e_ref[0, z + shift + 1, rows, :], e_ref[1, z + shift + 1, rows, :],
                )
                for i in range(3):
                    out[i, z + 1, rows, :] = new[i]
            return 0

        lax.fori_loop(0, NZ, body, 0, unroll=2)

    def main_curl(h_ref, z, r, strip):
        rows, back_rows = slice(r, r + 8), slice(r - 1, r + 7)
        far = 123 - 8 * z
        hx, hy, hz = (h_ref[i, z + 1, rows, :] for i in range(3))
        return curl(
            hx, hy, hz,
            jnp.where(lane == 0, pltpu.roll(strip[0, rows, :], far, 1), pltpu.roll(hx, 1, 1)),
            jnp.where(lane == 0, pltpu.roll(strip[2, rows, :], far, 1), pltpu.roll(hz, 1, 1)),
            h_ref[1, z + 1, back_rows, :], h_ref[2, z + 1, back_rows, :],
            h_ref[0, z, rows, :], h_ref[1, z, rows, :],
        )

    main_h(eh, 1, eh, 3, wide, h1, (6, 14, 22))

    def first_e(z, _):
        for r in (7, 15, 23):
            rows = slice(r, r + 8)
            turn = main_curl(h1, z, r, sh1)
            d = ad[3, z, rows, :]
            for i in range(3):
                e1[i, z, rows, :] = ad[i, z, rows, :] + d * turn[i]
        return 0

    lax.fori_loop(0, NZ, first_e, 0, unroll=2)
    main_h(e1, 0, h1, 0, se1, h2, (7, 15, 23))
    h_write = pltpu.make_async_copy(h2.at[:, inside, TOP:END, :], h_out, out_sem.at[0])
    h_write.start()

    def second_e(z, _):
        for b in (0, 8):
            rows, here = slice(TOP + b, TOP + b + 8), slice(b, b + 8)
            turn = main_curl(h2, z, TOP + b, sh2)
            d, factor = ad[3, z, rows, :], keep[z, here, :]
            for i in range(3):
                e2[i, z, here, :] = factor * e1[i, z, rows, :] + d * turn[i] + late[i, z, here, :]
        return 0

    lax.fori_loop(0, NZ, second_e, 0, unroll=2)
    e_write = pltpu.make_async_copy(e2, e_out, out_sem.at[1])
    e_write.start()
    for c in sends:
        c.wait_send()
    h_write.wait()
    e_write.wait()


def body(e_field, h_field, pole_now, pole_prev, material, eps_inf, resonance, damping, strength):
    anywhere = pl.BlockSpec(memory_space=pl.ANY)
    scalars = pl.BlockSpec(memory_space=pltpu.SMEM)
    f32 = jnp.float32
    block = jax.ShapeDtypeStruct(e_field.shape, f32)
    return pl.pallas_call(
        kernel,
        out_shape=(block, block),
        in_specs=[anywhere] * 5 + [scalars] * 4,
        out_specs=(anywhere, anywhere),
        scratch_shapes=[
            pltpu.VMEM((6, NZ + 2, 40, LANES), f32),
            pltpu.VMEM((4, NZ, 40, LANES), f32),
            pltpu.VMEM(pole_now.shape, f32),
            pltpu.VMEM(pole_prev.shape, f32),
            pltpu.VMEM(material.shape, jnp.int32),
            pltpu.VMEM((11, 4) + TILE, f32),
            pltpu.VMEM((NZ, ROWS, LANES), f32),
            pltpu.VMEM((3, NZ, ROWS, LANES), f32),
            pltpu.VMEM((3, NZ + 1, 40, LANES), f32),
            pltpu.VMEM((3, NZ + 1, 40, LANES), f32),
            pltpu.VMEM((3, NZ + 1, 40, LANES), f32),
            pltpu.VMEM((3, NZ, ROWS, LANES), f32),
            pltpu.VMEM((3, 10, 40, LANES), f32),
            pltpu.VMEM((10, 40, LANES), f32),
            pltpu.VMEM((3, 40, LANES), f32),
            pltpu.VMEM((3, 40, LANES), f32),
            pltpu.VMEM((3, 40, LANES), f32),
            pltpu.SemaphoreType.DMA((5,)),
            pltpu.SemaphoreType.DMA((14,)),
            pltpu.SemaphoreType.DMA((14,)),
            pltpu.SemaphoreType.DMA((2,)),
        ],
        compiler_params=pltpu.CompilerParams(
            collective_id=0, has_side_effects=True, vmem_limit_bytes=48 * 1024 * 1024
        ),
    )(e_field, h_field, pole_now, pole_prev, material, eps_inf, resonance, damping, strength)


def solution(mesh):
    field = P(None, None, "gx", "gy")
    pole = P(None, None, None, "gx", "gy")
    in_specs = (field, field, pole, pole, P(None, "gx", "gy"), P(), P(), P(), P())
    return jax.shard_map(
        body, mesh=mesh, in_specs=in_specs, out_specs=(field, field), check_vma=False
    )
```

time: 77.3 us -> 38.7 us (0.50)
  the two profiles are of different devices: /device:TPU:1 before, /device:TPU:14 now
where the time goes in v1:
time: 38.7 us; the launch traced here: 38.4 us
  Pallas kernels  29 us (75%)
  local copies, waits for them, and re-layouts  8.76 us (23%)
  between operations  0.66 us (2%)
    pallas_call x1, Pallas kernels, body(): pl.pallas_call(kernel, out_shape=(block, block), in_specs=[anywhere] * 5...  29 us
    unnamed x21, local copies, waits for them, and re-layouts  8.76 us

profile of v1, /device:TPU:14, one launch (start us, length us, event | category | flops | bytes accessed | tf_op | source)
XLA Modules:
  0.0 38.4 jit_solution(12363759114518896010)
XLA Ops:
  0.6 0.0 copy-start.6
  0.6 0.8 %copy.11.res_ref = f32[4,2]{1,0:T(4,128)S(1)} copy(f32[4,2]{0,1:T(2,128)} %param.15) | data formatting | bytes 64 | tf_op args[6]
  1.4 0.0 copy-done.6
  1.4 0.0 copy-start.7
  1.4 0.1 copy.12.damp_ref
  1.5 0.6 %copy-done.7 = f32[4,2]{0,1:T(2,128)S(1)} copy-done((f32[4,2]{0,1:T(2,128)S(1)}, f32[4,2]{0,1:T(2,128)}, u32[]{:S(2)}) %copy-start.7) | copy-done | bytes 56
  2.1 0.0 copy-start.5
  2.1 0.1 copy.13.str_ref
  2.2 0.6 %copy-done.5 = f32[4]{0:T(128)S(1)} copy-done((f32[4]{0:T(128)S(1)}, f32[4]{0:T(128)}, u32[]{:S(2)}) %copy-start.5) | copy-done | bytes 40
  2.7 0.0 copy-start
  2.8 1.1 %copy-done = f32[2,3,16,16,128]{4,3,2,1,0:T(8,128)S(1)} copy-done((f32[2,3,16,16,128]{4,3,2,1,0:T(8,128)S(1)}, f32[2,3,16,16,128]{4,3,2,1,0:T(8,128)}, u32[]{:S(2)}) %copy-start) | copy-done | bytes 786456
  3.9 0.0 copy-start.1
  3.9 1.1 %copy-done.1 = f32[2,3,16,16,128]{4,3,2,1,0:T(8,128)S(1)} copy-done((f32[2,3,16,16,128]{4,3,2,1,0:T(8,128)S(1)}, f32[2,3,16,16,128]{4,3,2,1,0:T(8,128)}, u32[]{:S(2)}) %copy-start.1) | copy-done | bytes 786456
  5.0 0.0 copy-start.2
  5.0 1.0 %copy-done.2 = f32[3,16,16,128]{3,2,1,0:T(8,128)S(1)} copy-done((f32[3,16,16,128]{3,2,1,0:T(8,128)S(1)}, f32[3,16,16,128]{3,2,1,0:T(8,128)}, u32[]{:S(2)}) %copy-start.2) | copy-done | bytes 393240
  6.0 0.0 copy-start.3
  6.0 1.0 %copy-done.3 = f32[3,16,16,128]{3,2,1,0:T(8,128)S(1)} copy-done((f32[3,16,16,128]{3,2,1,0:T(8,128)S(1)}, f32[3,16,16,128]{3,2,1,0:T(8,128)}, u32[]{:S(2)}) %copy-start.3) | copy-done | bytes 393240
  7.0 0.0 copy-start.4
  7.0 0.9 %copy-done.4 = s32[16,16,128]{2,1,0:T(8,128)S(1)} copy-done((s32[16,16,128]{2,1,0:T(8,128)S(1)}, s32[16,16,128]{2,1,0:T(8,128)}, u32[]{:S(2)}) %copy-start.4) | copy-done | bytes 131096
  7.9 29.0 %shard_map.104 = (f32[3,16,16,128]{3,2,1,0:T(8,128)S(1)}, f32[3,16,16,128]{3,2,1,0:T(8,128)S(1)}) custom-call(f32[3,16,16,128]{3,2,1,0:T(8,128)S(1)} %copy-done.2, f32[3,16,16,128]{3,2,1,0:T(8,128)S(1)} %copy-done.3, f32[2,3,16,16,128]{4,3,2,1,0:T(8,128)S(1)} %copy-done, f32[2,3,16,16,128]{4,3,2,1,0:T(8,128)S(1)} %copy-done.1, s32[16,16,128]{2,1,0:T(8,128)S(1)} %copy-done.4, ...), custom_call_target="tpu_custom_call" | custom-call | tf_op jit(solution)/shard_map/pallas_call | solution.py:285
  36.9 0.7 %copy.16 = f32[3,16,16,128]{3,2,1,0:T(8,128)} copy(f32[3,16,16,128]{3,2,1,0:T(8,128)S(1)} %get-tuple-element.4) | data formatting | bytes 786432
  37.6 0.7 %copy.17 = f32[3,16,16,128]{3,2,1,0:T(8,128)} copy(f32[3,16,16,128]{3,2,1,0:T(8,128)S(1)} %get-tuple-element.5) | data formatting | bytes 786432
Async XLA Ops:
  0.6 0.8 %copy-start.6 = (f32[4,2]{0,1:T(2,128)S(1)}, f32[4,2]{0,1:T(2,128)}, u32[]{:S(2)}) copy-start(f32[4,2]{0,1:T(2,128)} %param.16) | copy-start | bytes 100
  1.4 0.7 %copy-start.7 = (f32[4,2]{0,1:T(2,128)S(1)}, f32[4,2]{0,1:T(2,128)}, u32[]{:S(2)}) copy-start(f32[4,2]{0,1:T(2,128)} %param.17) | copy-start | bytes 100
  2.1 0.7 %copy-start.5 = (f32[4]{0:T(128)S(1)}, f32[4]{0:T(128)}, u32[]{:S(2)}) copy-start(f32[4]{0:T(128)} %eps_ref.1) | copy-start | bytes 52
  2.7 1.1 %copy-start = (f32[2,3,16,16,128]{4,3,2,1,0:T(8,128)S(1)}, f32[2,3,16,16,128]{4,3,2,1,0:T(8,128)}, u32[]{:S(2)}) copy-start(f32[2,3,16,16,128]{4,3,2,1,0:T(8,128)} %now_hbm.1) | copy-start | bytes 2359300
  3.9 1.1 %copy-start.1 = (f32[2,3,16,16,128]{4,3,2,1,0:T(8,128)S(1)}, f32[2,3,16,16,128]{4,3,2,1,0:T(8,128)}, u32[]{:S(2)}) copy-start(f32[2,3,16,16,128]{4,3,2,1,0:T(8,128)} %prev_hbm.1) | copy-start | bytes 2359300
  5.0 1.0 %copy-start.2 = (f32[3,16,16,128]{3,2,1,0:T(8,128)S(1)}, f32[3,16,16,128]{3,2,1,0:T(8,128)}, u32[]{:S(2)}) copy-start(f32[3,16,16,128]{3,2,1,0:T(8,128)} %e_hbm.1) | copy-start | bytes 1179652
  6.0 1.0 %copy-start.3 = (f32[3,16,16,128]{3,2,1,0:T(8,128)S(1)}, f32[3,16,16,128]{3,2,1,0:T(8,128)}, u32[]{:S(2)}) copy-start(f32[3,16,16,128]{3,2,1,0:T(8,128)} %h_hbm.1) | copy-start | bytes 1179652
  7.0 0.9 %copy-start.4 = (s32[16,16,128]{2,1,0:T(8,128)S(1)}, s32[16,16,128]{2,1,0:T(8,128)}, u32[]{:S(2)}) copy-start(s32[16,16,128]{2,1,0:T(8,128)} %mat_hbm.1) | copy-start | bytes 393220

commit v2 on v1

--- a/solution.py
+++ b/solution.py
@@ -22,9 +22,9 @@
         c3_sum = jnp.zeros(TILE, jnp.float32)
         r = jnp.zeros(TILE, jnp.float32)
         for k in range(2):
-            res = jnp.full(TILE, res_ref[m, k])
-            damp = jnp.full(TILE, damp_ref[m, k])
-            gain = jnp.full(TILE, str_ref[m, k])
+            res = jnp.full(TILE, res_ref[k, m])
+            damp = jnp.full(TILE, damp_ref[k, m])
+            gain = jnp.full(TILE, str_ref[k, m])
             if m == 3:
                 gain = jnp.zeros(TILE, jnp.float32)
             w = res * res * (DT * DT)
@@ -46,10 +46,11 @@
 
 
 def kernel(
-    e_hbm, h_hbm, now_hbm, prev_hbm, mat_hbm, eps_ref, res_ref, damp_ref, str_ref,
+    e_hbm, h_hbm, now_hbm, prev_hbm, mat_hbm, eps_hbm, res_hbm, damp_hbm, str_hbm,
     e_out, h_out,
-    eh, ad, now, prev, mat, tables, keep, late, h1, e1, h2, e2, strips, wide, sh1, se1, sh2,
-    load_sem, send_sem, recv_sem, out_sem,
+    eps_ref, res_ref, damp_ref, str_ref,
+    eh, ad, now, prev, mat, tables, keep, late, h1, e1, h2, strips, wide, sh1, se1, sh2,
+    load_sem, send_sem, recv_sem,
 ):
     gx, gy = lax.axis_index("gx"), lax.axis_index("gy")
     nx, ny = lax.axis_size("gx"), lax.axis_size("gy")
@@ -66,8 +67,16 @@
     barrier = pltpu.get_barrier_semaphore()
     for d in ((xp, gy), (xn, gy), (gx, yp), (gx, yn), (xp, yp), (xp, yn), (xn, yp), (xn, yn)):
         pl.semaphore_signal(barrier, inc=1, device_id=d, device_id_type=MESH)
-    for c in loads:
+    small = [
+        pltpu.make_async_copy(src, dst, load_sem.at[5 + i])
+        for i, (src, dst) in enumerate(
+            ((eps_hbm, eps_ref), (res_hbm, res_ref), (damp_hbm, damp_ref), (str_hbm, str_ref))
+        )
+    ]
+    for c in small + loads:
         c.start()
+    for c in small:
+        c.wait()
     fill_tables(tables, eps_ref, res_ref, damp_ref, str_ref)
     zero = jnp.zeros((40, LANES), jnp.float32)
     for c in range(3):
@@ -256,38 +265,41 @@
 
     lax.fori_loop(0, NZ, first_e, 0, unroll=2)
     main_h(e1, 0, h1, 0, se1, h2, (7, 15, 23))
-    h_write = pltpu.make_async_copy(h2.at[:, inside, TOP:END, :], h_out, out_sem.at[0])
-    h_write.start()
-
     def second_e(z, _):
         for b in (0, 8):
             rows, here = slice(TOP + b, TOP + b + 8), slice(b, b + 8)
             turn = main_curl(h2, z, TOP + b, sh2)
             d, factor = ad[3, z, rows, :], keep[z, here, :]
             for i in range(3):
-                e2[i, z, here, :] = factor * e1[i, z, rows, :] + d * turn[i] + late[i, z, here, :]
+                h_out[i, z, here, :] = h2[i, z + 1, rows, :]
+                e_out[i, z, here, :] = factor * e1[i, z, rows, :] + d * turn[i] + late[i, z, here, :]
         return 0
 
     lax.fori_loop(0, NZ, second_e, 0, unroll=2)
-    e_write = pltpu.make_async_copy(e2, e_out, out_sem.at[1])
-    e_write.start()
     for c in sends:
         c.wait_send()
-    h_write.wait()
-    e_write.wait()
 
 
 def body(e_field, h_field, pole_now, pole_prev, material, eps_inf, resonance, damping, strength):
-    anywhere = pl.BlockSpec(memory_space=pl.ANY)
-    scalars = pl.BlockSpec(memory_space=pltpu.SMEM)
+    hbm = pl.BlockSpec(memory_space=pltpu.HBM)
+    vmem = pl.BlockSpec(memory_space=pltpu.VMEM)
     f32 = jnp.float32
-    block = jax.ShapeDtypeStruct(e_field.shape, f32)
+    block = pltpu.VMEM(e_field.shape, f32)
+    operands = (
+        e_field, h_field, pole_now, pole_prev, material,
+        eps_inf, resonance.T, damping.T, strength.T,
+    )
+    operands = [pltpu.with_memory_space_constraint(x, pltpu.HBM) for x in operands]
     return pl.pallas_call(
         kernel,
         out_shape=(block, block),
-        in_specs=[anywhere] * 5 + [scalars] * 4,
-        out_specs=(anywhere, anywhere),
+        in_specs=[hbm] * 9,
+        out_specs=(vmem, vmem),
         scratch_shapes=[
+            pltpu.SMEM((4,), f32),
+            pltpu.SMEM((2, 4), f32),
+            pltpu.SMEM((2, 4), f32),
+            pltpu.SMEM((2, 4), f32),
             pltpu.VMEM((6, NZ + 2, 40, LANES), f32),
             pltpu.VMEM((4, NZ, 40, LANES), f32),
             pltpu.VMEM(pole_now.shape, f32),
@@ -299,21 +311,19 @@
             pltpu.VMEM((3, NZ + 1, 40, LANES), f32),
             pltpu.VMEM((3, NZ + 1, 40, LANES), f32),
             pltpu.VMEM((3, NZ + 1, 40, LANES), f32),
-            pltpu.VMEM((3, NZ, ROWS, LANES), f32),
             pltpu.VMEM((3, 10, 40, LANES), f32),
             pltpu.VMEM((10, 40, LANES), f32),
             pltpu.VMEM((3, 40, LANES), f32),
             pltpu.VMEM((3, 40, LANES), f32),
             pltpu.VMEM((3, 40, LANES), f32),
-            pltpu.SemaphoreType.DMA((5,)),
+            pltpu.SemaphoreType.DMA((9,)),
             pltpu.SemaphoreType.DMA((14,)),
             pltpu.SemaphoreType.DMA((14,)),
-            pltpu.SemaphoreType.DMA((2,)),
         ],
         compiler_params=pltpu.CompilerParams(
             collective_id=0, has_side_effects=True, vmem_limit_bytes=48 * 1024 * 1024
         ),
-    )(e_field, h_field, pole_now, pole_prev, material, eps_inf, resonance, damping, strength)
+    )(*operands)
 
 
 def solution(mesh):

time: 38.7 us -> 30.6 us (0.79)
  local copies, waits for them, and re-layouts: 8.76 us -> 1.49 us
  Pallas kernels: 29 us -> 28.3 us
    unnamed x21 -> x2, local copies, waits for them, and re-layouts: 8.76 us -> 1.49 us
    pallas_call x1, Pallas kernels: 29 us -> 28.3 us  [body(): pl.pallas_call(kernel, out_shape=(block, block), in_specs=[hbm] * 9, out_...]
where the time goes in v2:
time: 30.6 us; the launch traced here: 30.5 us
  Pallas kernels  28.3 us (92%)
  local copies, waits for them, and re-layouts  1.49 us (5%)
  between operations  0.64 us (2%)
    pallas_call x1, Pallas kernels, body(): pl.pallas_call(kernel, out_shape=(block, block), in_specs=[hbm] * 9, out_...  28.3 us
    unnamed x2, local copies, waits for them, and re-layouts  1.49 us

profile of v2, /device:TPU:14, one launch (start us, length us, event | category | flops | bytes accessed | tf_op | source)
XLA Modules:
  0.0 30.5 jit_solution(6904968114093701374)
XLA Ops:
  0.6 28.3 %shard_map.104 = (f32[3,16,16,128]{3,2,1,0:T(8,128)S(1)}, f32[3,16,16,128]{3,2,1,0:T(8,128)S(1)}) custom-call(f32[3,16,16,128]{3,2,1,0:T(8,128)} %e_hbm.1, f32[3,16,16,128]{3,2,1,0:T(8,128)} %h_hbm.1, f32[2,3,16,16,128]{4,3,2,1,0:T(8,128)} %now_hbm.1, f32[2,3,16,16,128]{4,3,2,1,0:T(8,128)} %prev_hbm.1, s32[16,16,128]{2,1,0:T(8,128)} %mat_hbm.1, f32[4]{0:T(128)} %eps_hbm.1, ...), custom_call_target="tpu_custom_call" | custom-call | tf_op jit(solution)/shard_map/pallas_call | solution.py:293
  29.0 0.7 %copy.13 = f32[3,16,16,128]{3,2,1,0:T(8,128)} copy(f32[3,16,16,128]{3,2,1,0:T(8,128)S(1)} %get-tuple-element.2) | data formatting | bytes 786432
  29.7 0.7 %copy.14 = f32[3,16,16,128]{3,2,1,0:T(8,128)} copy(f32[3,16,16,128]{3,2,1,0:T(8,128)S(1)} %get-tuple-element.3) | data formatting | bytes 786432

commit v3 on v2

--- a/solution.py
+++ b/solution.py
@@ -49,72 +49,110 @@
     e_hbm, h_hbm, now_hbm, prev_hbm, mat_hbm, eps_hbm, res_hbm, damp_hbm, str_hbm,
     e_out, h_out,
     eps_ref, res_ref, damp_ref, str_ref,
-    eh, ad, now, prev, mat, tables, keep, late, h1, e1, h2, strips, wide, sh1, se1, sh2,
-    load_sem, send_sem, recv_sem,
+    eh, ad, now, prev, mat, tables, keep, late, h1, e1, h2,
+    strips, wide, sh1, se1, sh2, load_sem, send_sem, recv_sem,
 ):
     gx, gy = lax.axis_index("gx"), lax.axis_index("gy")
     nx, ny = lax.axis_size("gx"), lax.axis_size("gy")
     xp, xn = lax.rem(gx + nx - 1, nx), lax.rem(gx + 1, nx)
     yp, yn = lax.rem(gy + ny - 1, ny), lax.rem(gy + 1, ny)
 
+    barrier = pltpu.get_barrier_semaphore()
+    for d in ((xp, yp), (xp, yn), (xn, yp), (xn, yn), (gx, yp), (gx, yn), (xp, gy), (xn, gy)):
+        pl.semaphore_signal(barrier, inc=1, device_id=d, device_id_type=MESH)
     loads = [
-        pltpu.make_async_copy(e_hbm, eh.at[0:3, 1 : NZ + 1, TOP:END, :], load_sem.at[0]),
-        pltpu.make_async_copy(h_hbm, eh.at[3:6, 1 : NZ + 1, TOP:END, :], load_sem.at[1]),
-        pltpu.make_async_copy(mat_hbm, mat, load_sem.at[2]),
-        pltpu.make_async_copy(now_hbm, now, load_sem.at[3]),
-        pltpu.make_async_copy(prev_hbm, prev, load_sem.at[4]),
+        pltpu.make_async_copy(src, dst, load_sem.at[i])
+        for i, (src, dst) in enumerate((
+            (e_hbm, eh.at[0:3, 1 : NZ + 1, TOP:END, :]),
+            (h_hbm, eh.at[3:6, 1 : NZ + 1, TOP:END, :]),
+            (mat_hbm, mat),
+            (now_hbm, now),
+            (prev_hbm, prev),
+            (eps_hbm, eps_ref),
+            (res_hbm, res_ref),
+            (damp_hbm, damp_ref),
+            (str_hbm, str_ref),
+        ))
     ]
-    barrier = pltpu.get_barrier_semaphore()
-    for d in ((xp, gy), (xn, gy), (gx, yp), (gx, yn), (xp, yp), (xp, yn), (xn, yp), (xn, yn)):
-        pl.semaphore_signal(barrier, inc=1, device_id=d, device_id_type=MESH)
-    small = [
-        pltpu.make_async_copy(src, dst, load_sem.at[5 + i])
-        for i, (src, dst) in enumerate(
-            ((eps_hbm, eps_ref), (res_hbm, res_ref), (damp_hbm, damp_ref), (str_hbm, str_ref))
-        )
+    for c in loads:
+        c.start()
+    pl.semaphore_wait(barrier, 8)
+
+    def send(index, src, dst, device):
+        c = pltpu.make_async_remote_copy(
+            src_ref=src, dst_ref=dst, send_sem=send_sem.at[index], recv_sem=recv_sem.at[index],
+            device_id=device, device_id_type=MESH,
+        )
+        c.start()
+        return c
+
+    inside = pl.ds(1, NZ)
+    first = [
+        send(0, e_hbm.at[:, :, 14:16, :], eh.at[0:3, inside, 6:8, :], (xn, gy)),
+        send(1, h_hbm.at[:, :, 14:16, :], eh.at[3:6, inside, 6:8, :], (xn, gy)),
+        send(2, e_hbm.at[:, :, 0:2, :], eh.at[0:3, inside, 24:26, :], (xp, gy)),
+        send(3, h_hbm.at[:, :, 0:1, :], eh.at[3:6, inside, 24:25, :], (xp, gy)),
     ]
-    for c in small + loads:
-        c.start()
-    for c in small:
-        c.wait()
-    fill_tables(tables, eps_ref, res_ref, damp_ref, str_ref)
     zero = jnp.zeros((40, LANES), jnp.float32)
     for c in range(3):
         eh[c, NZ + 1] = zero
         e1[c, NZ] = zero
         h1[c, 0] = zero
         h2[c, 0] = zero
-    pl.semaphore_wait(barrier, 8)
-
-    def send(index, src, dst, device):
-        c = pltpu.make_async_remote_copy(
-            src_ref=src, dst_ref=dst, send_sem=send_sem.at[index], recv_sem=recv_sem.at[index],
-            device_id=device, device_id_type=MESH,
-        )
-        c.start()
-        return c
-
-    inside = pl.ds(1, NZ)
-    sends = [
-        send(0, e_hbm.at[:, :, 14:16, :], eh.at[0:3, inside, 6:8, :], (xn, gy)),
-        send(1, h_hbm.at[:, :, 14:16, :], eh.at[3:6, inside, 6:8, :], (xn, gy)),
-        send(2, e_hbm.at[:, :, 0:2, :], eh.at[0:3, inside, 24:26, :], (xp, gy)),
-        send(3, h_hbm.at[:, :, 0:1, :], eh.at[3:6, inside, 24:25, :], (xp, gy)),
+
+    lane = lax.broadcasted_iota(jnp.int32, TILE, 1)
+    slot = lane & 7
+
+    def pack(items):
+        for b in (0, 8):
+            rows = slice(TOP + b, TOP + b + 8)
+            for tile in sorted({i // 4 for i in items}):
+                group = [i for i in items if i // 4 == tile]
+                right = jnp.zeros(TILE, jnp.float32)
+                left = jnp.zeros(TILE, jnp.float32)
+                for z in range(NZ):
+                    for i in group:
+                        p = 8 * z + 2 * (i % 4)
+                        f = eh[i, z + 1, rows, :] if i < 6 else ad[i - 8, z, rows, :]
+                        f = pltpu.roll(f, p + 2, 1)
+                        right = jnp.where(lane // 2 == p // 2, f, right)
+                        left = jnp.where(lane // 2 == (p // 2 + 1) % 64, f, left)
+                strips[0, tile, rows, :] = right
+                strips[1, tile, rows, :] = left
+
+    loads[0].wait()
+    loads[1].wait()
+    pack(range(6))
+    a, b = pl.ds(22, 2), pl.ds(8, 2)
+    low, high = pl.ds(6, 2), pl.ds(24, 2)
+    mid, part = pl.ds(TOP, ROWS), pl.ds(0, 2)
+    first += [
+        send(4, strips.at[0, part, a, :], strips.at[2, part, low, :], (xn, yn)),
+        send(5, strips.at[1, part, a, :], strips.at[3, part, low, :], (xn, yp)),
+        send(6, strips.at[0, part, b, :], strips.at[2, part, high, :], (xp, yn)),
+        send(7, strips.at[1, part, b, :], strips.at[3, part, high, :], (xp, yp)),
+        send(8, strips.at[0, part, mid, :], strips.at[2, part, mid, :], (gx, yn)),
+        send(9, strips.at[1, part, mid, :], strips.at[3, part, mid, :], (gx, yp)),
+        send(10, strips.at[0:2, part, a, :], strips.at[0:2, part, low, :], (xn, gy)),
+        send(11, strips.at[0:2, part, b, :], strips.at[0:2, part, high, :], (xp, gy)),
     ]
-    for c in loads:
+    for c in loads[5:]:
+        c.wait()
+    fill_tables(tables, eps_ref, res_ref, damp_ref, str_ref)
+    for c in loads[2:5]:
         c.wait()
 
     def local(z, _):
         for b in (0, 8):
             kind = mat[z, b : b + 8, :]
-            low = (kind & 1) == 1
-            high = kind >= 2
+            odd = (kind & 1) == 1
+            upper = kind >= 2
 
             def value(i):
                 return jnp.where(
-                    high,
-                    jnp.where(low, tables[i, 3], tables[i, 2]),
-                    jnp.where(low, tables[i, 1], tables[i, 0]),
+                    upper,
+                    jnp.where(odd, tables[i, 3], tables[i, 2]),
+                    jnp.where(odd, tables[i, 1], tables[i, 0]),
                 )
 
             e, d, g0, g1, w0, w1, p0, p1, q0, q1, r = [value(i) for i in range(11)]
@@ -129,52 +167,34 @@
                 late[c, z, b : b + 8, :] = (r * f + (p0 * n0 + p1 * n1)) + (q0 * m0 + q1 * m1)
         return 0
 
-    lax.fori_loop(0, NZ, local, 0)
-
-    lane = lax.broadcasted_iota(jnp.int32, TILE, 1)
-    group = lane // 8
-    slot = lane % 8
-
-    def pack(z, held):
-        mine = group == z
-        out = []
-        for i in range(10):
-            for b in (0, 8):
-                rows = slice(TOP + b, TOP + b + 8)
-                f = eh[i, z + 1, rows, :] if i < 6 else ad[i - 6, z, rows, :]
-                out.append(jnp.where(mine, pltpu.roll(f, 8 * z + 2, 1), held[len(out)]))
-        return tuple(out)
-
-    held = lax.fori_loop(0, NZ, pack, tuple(jnp.zeros(TILE, jnp.float32) for _ in range(20)))
-    for i in range(10):
-        for j in range(2):
-            strips[0, i, TOP + 8 * j : TOP + 8 * j + 8, :] = held[2 * i + j]
-
-    own = strips.at[0]
-    sends += [
-        send(4, own.at[:, TOP:END, :], strips.at[1, :, TOP:END, :], (gx, yn)),
-        send(5, own.at[:, TOP:END, :], strips.at[2, :, TOP:END, :], (gx, yp)),
-        send(6, ad.at[:, :, 23:24, :], ad.at[:, :, 7:8, :], (xn, gy)),
-        send(7, ad.at[:, :, 8:9, :], ad.at[:, :, 24:25, :], (xp, gy)),
-        send(8, own.at[:, 22:24, :], strips.at[0, :, 6:8, :], (xn, gy)),
-        send(9, own.at[:, 8:10, :], strips.at[0, :, 24:26, :], (xp, gy)),
-        send(10, own.at[:, 22:24, :], strips.at[1, :, 6:8, :], (xn, yn)),
-        send(11, own.at[:, 22:24, :], strips.at[2, :, 6:8, :], (xn, yp)),
-        send(12, own.at[:, 8:10, :], strips.at[1, :, 24:26, :], (xp, yn)),
-        send(13, own.at[:, 8:10, :], strips.at[2, :, 24:26, :], (xp, yp)),
+    lax.fori_loop(0, NZ, local, 0, unroll=8)
+    pack(range(8, 12))
+    second = [
+        send(12, strips.at[1, 2, pl.ds(23, 1), :], strips.at[3, 2, pl.ds(7, 1), :], (xn, yp)),
+        send(13, strips.at[0, 2, pl.ds(8, 1), :], strips.at[2, 2, pl.ds(24, 1), :], (xp, yn)),
+        send(14, strips.at[0, 2, mid, :], strips.at[2, 2, mid, :], (gx, yn)),
+        send(15, strips.at[1, 2, mid, :], strips.at[3, 2, mid, :], (gx, yp)),
+        send(16, ad.at[:, :, 23:24, :], ad.at[:, :, 7:8, :], (xn, gy)),
+        send(17, ad.at[1:4, :, 8:9, :], ad.at[1:4, :, 24:25, :], (xp, gy)),
     ]
-    for c in sends:
+
+    def widen(items, starts):
+        for r in starts:
+            rows = slice(r, r + 8)
+            for tile in sorted({i // 4 for i in items}):
+                right, left = strips[0, tile, rows, :], pltpu.roll(strips[1, tile, rows, :], 4, 1)
+                before, after = pltpu.roll(strips[2, tile, rows, :], 4, 1), strips[3, tile, rows, :]
+                for i in items:
+                    if i // 4 != tile:
+                        continue
+                    p = 2 * (i % 4)
+                    q = (lane + 8 - p) & 7
+                    f = jnp.where(q < 4, jnp.where(q < 2, right, after), jnp.where(q < 6, before, left))
+                    wide[i, rows, :] = pltpu.roll(f, LANES - p, 1) if p else f
+
+    for c in first:
         c.wait_recv()
-
-    for i in range(10):
-        for r in (6, 14, 22):
-            rows = slice(r, r + 8)
-            me, before, after = strips[0, i, rows, :], strips[1, i, rows, :], strips[2, i, rows, :]
-            wide[i, rows, :] = jnp.where(
-                slot < 4,
-                jnp.where(slot < 2, me, after),
-                pltpu.roll(jnp.where(slot < 2, before, me), 4, 1),
-            )
+    widen(range(6), (6, 14, 22))
 
     def ahead_z(f):
         return jnp.where(lane < 120, pltpu.roll(f, 120, 1), 0.0)
@@ -207,19 +227,6 @@
             )
             for i in range(3):
                 out[i, rows, :] = new[i]
-
-    strip_h(wide, wide, 3, sh1, (6, 14, 22))
-    for r in (7, 15, 23):
-        rows, back_rows = slice(r, r + 8), slice(r - 1, r + 7)
-        hx, hy, hz = (sh1[i, rows, :] for i in range(3))
-        turn = curl(
-            hx, hy, hz, pltpu.roll(hx, 1, 1), pltpu.roll(hz, 1, 1),
-            sh1[1, back_rows, :], sh1[2, back_rows, :], behind_z(hx), behind_z(hy),
-        )
-        d = wide[9, rows, :]
-        for i in range(3):
-            se1[i, rows, :] = wide[6 + i, rows, :] + d * turn[i]
-    strip_h(se1, sh1, 0, sh2, (7, 15, 23))
 
     def main_h(e_ref, shift, h_ref, h_base, strip, out, starts):
         def body(z, _):
@@ -238,7 +245,7 @@
                     out[i, z + 1, rows, :] = new[i]
             return 0
 
-        lax.fori_loop(0, NZ, body, 0, unroll=2)
+        lax.fori_loop(0, NZ, body, 0, unroll=NZ)
 
     def main_curl(h_ref, z, r, strip):
         rows, back_rows = slice(r, r + 8), slice(r - 1, r + 7)
@@ -252,7 +259,22 @@
             h_ref[0, z, rows, :], h_ref[1, z, rows, :],
         )
 
+    strip_h(wide, wide, 3, sh1, (6, 14, 22))
     main_h(eh, 1, eh, 3, wide, h1, (6, 14, 22))
+    for c in second:
+        c.wait_recv()
+    widen(range(8, 12), (7, 15, 23))
+    for r in (7, 15, 23):
+        rows, back_rows = slice(r, r + 8), slice(r - 1, r + 7)
+        hx, hy, hz = (sh1[i, rows, :] for i in range(3))
+        turn = curl(
+            hx, hy, hz, pltpu.roll(hx, 1, 1), pltpu.roll(hz, 1, 1),
+            sh1[1, back_rows, :], sh1[2, back_rows, :], behind_z(hx), behind_z(hy),
+        )
+        d = wide[11, rows, :]
+        for i in range(3):
+            se1[i, rows, :] = wide[8 + i, rows, :] + d * turn[i]
+    strip_h(se1, sh1, 0, sh2, (7, 15, 23))
 
     def first_e(z, _):
         for r in (7, 15, 23):
@@ -263,7 +285,7 @@
                 e1[i, z, rows, :] = ad[i, z, rows, :] + d * turn[i]
         return 0
 
-    lax.fori_loop(0, NZ, first_e, 0, unroll=2)
+    lax.fori_loop(0, NZ, first_e, 0, unroll=NZ)
     main_h(e1, 0, h1, 0, se1, h2, (7, 15, 23))
     def second_e(z, _):
         for b in (0, 8):
@@ -275,9 +297,17 @@
                 e_out[i, z, here, :] = factor * e1[i, z, rows, :] + d * turn[i] + late[i, z, here, :]
         return 0
 
-    lax.fori_loop(0, NZ, second_e, 0, unroll=2)
-    for c in sends:
+    lax.fori_loop(0, NZ, second_e, 0, unroll=NZ)
+    for c in first + second:
         c.wait_send()
+
+
+def write_out(e_ref, h_ref, e_out, h_out, sem):
+    copies = [pltpu.make_async_copy(e_ref, e_out, sem.at[0]), pltpu.make_async_copy(h_ref, h_out, sem.at[1])]
+    for c in copies:
+        c.start()
+    for c in copies:
+        c.wait()
 
 
 def body(e_field, h_field, pole_now, pole_prev, material, eps_inf, resonance, damping, strength):
@@ -290,7 +320,7 @@
         eps_inf, resonance.T, damping.T, strength.T,
     )
     operands = [pltpu.with_memory_space_constraint(x, pltpu.HBM) for x in operands]
-    return pl.pallas_call(
+    fields = pl.pallas_call(
         kernel,
         out_shape=(block, block),
         in_specs=[hbm] * 9,
@@ -311,19 +341,27 @@
             pltpu.VMEM((3, NZ + 1, 40, LANES), f32),
             pltpu.VMEM((3, NZ + 1, 40, LANES), f32),
             pltpu.VMEM((3, NZ + 1, 40, LANES), f32),
-            pltpu.VMEM((3, 10, 40, LANES), f32),
-            pltpu.VMEM((10, 40, LANES), f32),
+            pltpu.VMEM((4, 3, 40, LANES), f32),
+            pltpu.VMEM((12, 40, LANES), f32),
             pltpu.VMEM((3, 40, LANES), f32),
             pltpu.VMEM((3, 40, LANES), f32),
             pltpu.VMEM((3, 40, LANES), f32),
             pltpu.SemaphoreType.DMA((9,)),
-            pltpu.SemaphoreType.DMA((14,)),
-            pltpu.SemaphoreType.DMA((14,)),
+            pltpu.SemaphoreType.DMA((18,)),
+            pltpu.SemaphoreType.DMA((18,)),
         ],
         compiler_params=pltpu.CompilerParams(
             collective_id=0, has_side_effects=True, vmem_limit_bytes=48 * 1024 * 1024
         ),
     )(*operands)
+    fields = [pltpu.with_memory_space_constraint(x, pltpu.VMEM) for x in fields]
+    return pl.pallas_call(
+        write_out,
+        out_shape=(pltpu.HBM(e_field.shape, f32),) * 2,
+        in_specs=[vmem, vmem],
+        out_specs=(hbm, hbm),
+        scratch_shapes=[pltpu.SemaphoreType.DMA((2,))],
+    )(*fields)
 
 
 def solution(mesh):

time: 30.6 us -> 23.9 us (0.78)
  the two profiles are of different devices: /device:TPU:14 before, /device:TPU:8 now
where the time goes in v3:
time: 23.9 us; the launch traced here: 23.8 us
  Pallas kernels  23.1 us (97%)
  between operations  0.64 us (3%)
    pallas_call x1, Pallas kernels, body(): pl.pallas_call(kernel, out_shape=(block, block), in_specs=[hbm] * 9, out_...  22.2 us
    pallas_call x1, Pallas kernels, body(): pl.pallas_call(write_out, out_shape=(pltpu.HBM(e_field.shape, f32),) * 2,...  0.89 us

profile of v3, /device:TPU:8, one launch (start us, length us, event | category | flops | bytes accessed | tf_op | source)
XLA Modules:
  0.0 23.8 jit_solution(13049652839788890825)
XLA Ops:
  0.6 22.2 %shard_map.104 = (f32[3,16,16,128]{3,2,1,0:T(8,128)S(1)}, f32[3,16,16,128]{3,2,1,0:T(8,128)S(1)}) custom-call(f32[3,16,16,128]{3,2,1,0:T(8,128)} %e_hbm.1, f32[3,16,16,128]{3,2,1,0:T(8,128)} %h_hbm.1, f32[2,3,16,16,128]{4,3,2,1,0:T(8,128)} %now_hbm.1, f32[2,3,16,16,128]{4,3,2,1,0:T(8,128)} %prev_hbm.1, s32[16,16,128]{2,1,0:T(8,128)} %mat_hbm.1, f32[4]{0:T(128)} %eps_hbm.1, ...), custom_call_target="tpu_custom_call" | custom-call | tf_op jit(solution)/shard_map/pallas_call | solution.py:323
  22.9 0.9 %shard_map.105 = (f32[3,16,16,128]{3,2,1,0:T(8,128)}, f32[3,16,16,128]{3,2,1,0:T(8,128)}) custom-call(f32[3,16,16,128]{3,2,1,0:T(8,128)S(1)} %get-tuple-element.4.e_ref, f32[3,16,16,128]{3,2,1,0:T(8,128)S(1)} %get-tuple-element.5.h_ref), custom_call_target="tpu_custom_call" | custom-call | tf_op jit(solution)/shard_map/pallas_call | solution.py:358

commit v4 on v3

--- a/solution.py
+++ b/solution.py
@@ -50,7 +50,8 @@
     e_out, h_out,
     eps_ref, res_ref, damp_ref, str_ref,
     eh, ad, now, prev, mat, tables, keep, late, h1, e1, h2,
-    strips, wide, sh1, se1, sh2, load_sem, send_sem, recv_sem,
+    strips, wide, sh1, se1, sh2, edge_e, edge_h, edge_new, outgo, income, ring,
+    load_sem, send_sem, recv_sem,
 ):
     gx, gy = lax.axis_index("gx"), lax.axis_index("gy")
     nx, ny = lax.axis_size("gx"), lax.axis_size("gy")
@@ -73,10 +74,13 @@
             (damp_hbm, damp_ref),
             (str_hbm, str_ref),
         ))
+    ] + [
+        pltpu.make_async_copy(field.at[:, :, row, :], edge.at[k, :, 8:24, :], load_sem.at[9 + 4 * j + k])
+        for j, (field, edge, rows) in enumerate(((e_hbm, edge_e, (0, 1, 14, 15)), (h_hbm, edge_h, (0, 14, 15))))
+        for k, row in enumerate(rows)
     ]
     for c in loads:
         c.start()
-    pl.semaphore_wait(barrier, 8)
 
     def send(index, src, dst, device):
         c = pltpu.make_async_remote_copy(
@@ -86,19 +90,16 @@
         c.start()
         return c
 
-    inside = pl.ds(1, NZ)
-    first = [
-        send(0, e_hbm.at[:, :, 14:16, :], eh.at[0:3, inside, 6:8, :], (xn, gy)),
-        send(1, h_hbm.at[:, :, 14:16, :], eh.at[3:6, inside, 6:8, :], (xn, gy)),
-        send(2, e_hbm.at[:, :, 0:2, :], eh.at[0:3, inside, 24:26, :], (xp, gy)),
-        send(3, h_hbm.at[:, :, 0:1, :], eh.at[3:6, inside, 24:25, :], (xp, gy)),
-    ]
     zero = jnp.zeros((40, LANES), jnp.float32)
     for c in range(3):
         eh[c, NZ + 1] = zero
         e1[c, NZ] = zero
         h1[c, 0] = zero
         h2[c, 0] = zero
+        for k in range(4):
+            edge_e[k, c, 24:32, :] = jnp.zeros(TILE, jnp.float32)
+        for k in range(2):
+            edge_new[k, c, 0:8, :] = jnp.zeros(TILE, jnp.float32)
 
     lane = lax.broadcasted_iota(jnp.int32, TILE, 1)
     slot = lane & 7
@@ -123,20 +124,7 @@
     loads[0].wait()
     loads[1].wait()
     pack(range(6))
-    a, b = pl.ds(22, 2), pl.ds(8, 2)
-    low, high = pl.ds(6, 2), pl.ds(24, 2)
-    mid, part = pl.ds(TOP, ROWS), pl.ds(0, 2)
-    first += [
-        send(4, strips.at[0, part, a, :], strips.at[2, part, low, :], (xn, yn)),
-        send(5, strips.at[1, part, a, :], strips.at[3, part, low, :], (xn, yp)),
-        send(6, strips.at[0, part, b, :], strips.at[2, part, high, :], (xp, yn)),
-        send(7, strips.at[1, part, b, :], strips.at[3, part, high, :], (xp, yp)),
-        send(8, strips.at[0, part, mid, :], strips.at[2, part, mid, :], (gx, yn)),
-        send(9, strips.at[1, part, mid, :], strips.at[3, part, mid, :], (gx, yp)),
-        send(10, strips.at[0:2, part, a, :], strips.at[0:2, part, low, :], (xn, gy)),
-        send(11, strips.at[0:2, part, b, :], strips.at[0:2, part, high, :], (xp, gy)),
-    ]
-    for c in loads[5:]:
+    for c in loads[5:9]:
         c.wait()
     fill_tables(tables, eps_ref, res_ref, damp_ref, str_ref)
     for c in loads[2:5]:
@@ -169,13 +157,72 @@
 
     lax.fori_loop(0, NZ, local, 0, unroll=8)
     pack(range(8, 12))
-    second = [
-        send(12, strips.at[1, 2, pl.ds(23, 1), :], strips.at[3, 2, pl.ds(7, 1), :], (xn, yp)),
-        send(13, strips.at[0, 2, pl.ds(8, 1), :], strips.at[2, 2, pl.ds(24, 1), :], (xp, yn)),
-        send(14, strips.at[0, 2, mid, :], strips.at[2, 2, mid, :], (gx, yn)),
-        send(15, strips.at[1, 2, mid, :], strips.at[3, 2, mid, :], (gx, yp)),
-        send(16, ad.at[:, :, 23:24, :], ad.at[:, :, 7:8, :], (xn, gy)),
-        send(17, ad.at[1:4, :, 8:9, :], ad.at[1:4, :, 24:25, :], (xp, gy)),
+    for c in loads[9:]:
+        c.wait()
+
+    def h_step(ex, ey, ez, hx, hy, hz, ex_y, ez_y, ey_x, ez_x, ex_z, ey_z):
+        return (
+            hx - DT * ((ez_y - ez) - (ey_z - ey)),
+            hy - DT * ((ex_z - ex) - (ez_x - ez)),
+            hz - DT * ((ey_x - ey) - (ex_y - ex)),
+        )
+
+    def curl(hx, hy, hz, hx_y, hz_y, hy_x, hz_x, hx_z, hy_z):
+        return (
+            (hz - hz_y) - (hy - hy_z),
+            (hx - hx_z) - (hz - hz_x),
+            (hy - hy_x) - (hx - hx_y),
+        )
+
+    span, up = slice(8, 24), slice(9, 25)
+    down = slice(7, 23)
+
+    def edge_step(here, there, h_here):
+        e = [edge_e[here, i, span, :] for i in range(3)]
+        ey_x, ez_x = (0.0, 0.0) if there is None else (edge_e[there, 1, span, :], edge_e[there, 2, span, :])
+        return h_step(
+            *e, *(edge_h[h_here, i, span, :] for i in range(3)),
+            pltpu.roll(e[0], 127, 1), pltpu.roll(e[2], 127, 1), ey_x, ez_x,
+            edge_e[here, 0, up, :], edge_e[here, 1, up, :],
+        )
+
+    end_h = edge_step(3, None, 2)
+    inner_h = edge_step(2, 3, 1)
+    start_h = edge_step(0, 1, 0)
+    for i in range(3):
+        edge_new[0, i, span, :] = end_h[i]
+        edge_new[1, i, span, :] = start_h[i]
+    hx, hy, hz = end_h
+    turn = curl(
+        hx, hy, hz, pltpu.roll(hx, 1, 1), pltpu.roll(hz, 1, 1), inner_h[1], inner_h[2],
+        edge_new[0, 0, down, :], edge_new[0, 1, down, :],
+    )
+    d = ad[3, :, 23, :]
+    outgo[0], outgo[1], outgo[5] = hy, hz, d
+    for i in range(3):
+        outgo[2 + i] = ad[i, :, 23, :] + d * turn[i]
+    hx, hy, hz = start_h
+    d = ad[3, :, 8, :]
+    outgo[6] = ad[1, :, 8, :] + d * ((hx - edge_new[1, 0, down, :]) - hz)
+    outgo[7] = ad[2, :, 8, :] + d * (hy - (hx - pltpu.roll(hx, 1, 1)))
+    outgo[8] = d
+
+    a, b = pl.ds(22, 2), pl.ds(8, 2)
+    low, high = pl.ds(6, 2), pl.ds(24, 2)
+    mid = pl.ds(TOP, ROWS)
+    pl.semaphore_wait(barrier, 8)
+    sends = [
+        send(0, strips.at[0, :, a, :], strips.at[2, :, low, :], (xn, yn)),
+        send(1, strips.at[1, :, a, :], strips.at[3, :, low, :], (xn, yp)),
+        send(2, strips.at[0, :, b, :], strips.at[2, :, high, :], (xp, yn)),
+        send(3, strips.at[1, :, b, :], strips.at[3, :, high, :], (xp, yp)),
+        send(4, strips.at[0, :, mid, :], strips.at[2, :, mid, :], (gx, yn)),
+        send(5, strips.at[1, :, mid, :], strips.at[3, :, mid, :], (gx, yp)),
+        send(6, strips.at[0:2, :, a, :], strips.at[0:2, :, low, :], (xn, gy)),
+        send(7, strips.at[0:2, :, b, :], strips.at[0:2, :, high, :], (xp, gy)),
+        send(8, e_hbm.at[1:3, :, 0:1, :], eh.at[1:3, 1 : NZ + 1, 24:25, :], (xp, gy)),
+        send(9, outgo.at[0:6], income.at[0:6], (xn, gy)),
+        send(10, outgo.at[6:9], income.at[6:9], (xp, gy)),
     ]
 
     def widen(items, starts):
@@ -192,29 +239,16 @@
                     f = jnp.where(q < 4, jnp.where(q < 2, right, after), jnp.where(q < 6, before, left))
                     wide[i, rows, :] = pltpu.roll(f, LANES - p, 1) if p else f
 
-    for c in first:
+    for c in sends:
         c.wait_recv()
     widen(range(6), (6, 14, 22))
+    widen(range(8, 12), (7, 15, 23))
 
     def ahead_z(f):
         return jnp.where(lane < 120, pltpu.roll(f, 120, 1), 0.0)
 
     def behind_z(f):
         return jnp.where(lane >= 8, pltpu.roll(f, 8, 1), 0.0)
-
-    def h_step(ex, ey, ez, hx, hy, hz, ex_y, ez_y, ey_x, ez_x, ex_z, ey_z):
-        return (
-            hx - DT * ((ez_y - ez) - (ey_z - ey)),
-            hy - DT * ((ex_z - ex) - (ez_x - ez)),
-            hz - DT * ((ey_x - ey) - (ex_y - ex)),
-        )
-
-    def curl(hx, hy, hz, hx_y, hz_y, hy_x, hz_x, hx_z, hy_z):
-        return (
-            (hz - hz_y) - (hy - hy_z),
-            (hx - hx_z) - (hz - hz_x),
-            (hy - hy_x) - (hx - hx_y),
-        )
 
     def strip_h(e_ref, h_ref, base, out, starts):
         for r in starts:
@@ -260,10 +294,6 @@
         )
 
     strip_h(wide, wide, 3, sh1, (6, 14, 22))
-    main_h(eh, 1, eh, 3, wide, h1, (6, 14, 22))
-    for c in second:
-        c.wait_recv()
-    widen(range(8, 12), (7, 15, 23))
     for r in (7, 15, 23):
         rows, back_rows = slice(r, r + 8), slice(r - 1, r + 7)
         hx, hy, hz = (sh1[i, rows, :] for i in range(3))
@@ -276,8 +306,41 @@
             se1[i, rows, :] = wide[8 + i, rows, :] + d * turn[i]
     strip_h(se1, sh1, 0, sh2, (7, 15, 23))
 
+    line = lane[0:1, :]
+    for k, r in enumerate((7, 24)):
+        for i in range(3):
+            f = se1[i, r : r + 1, :]
+            ring[i, k : k + 1, :] = jnp.where((line & 7) == 2, pltpu.roll(f, 124, 1), f)
+
+    def edge_lanes(f, i, k, z):
+        wrapped = pltpu.roll(ring[i, k : k + 1, :], 126 - 8 * z, 1)
+        return jnp.where((line == 0) | (line == 127), wrapped, f)
+
+    main_h(eh, 1, eh, 3, wide, h1, (8, 16))
+    at = slice(7, 8)
+    for z in range(NZ):
+        layer = slice(z, z + 1)
+        dhy = DT * eh[2, z + 1, 8:9, :]
+        dhz = -DT * eh[1, z + 1, 8:9, :]
+        dhy_z = dhy if z == 0 else dhy - DT * eh[2, z, 8:9, :]
+        h1[1, z + 1, at, :] = income[0, layer, :] + dhy
+        h1[2, z + 1, at, :] = jnp.where(
+            line == 127, pltpu.roll(sh1[2, at, :], 126 - 8 * z, 1), income[1, layer, :] + dhz
+        )
+        d = income[5, layer, :]
+        ex = income[2, layer, :] + d * ((dhz - pltpu.roll(dhz, 1, 1)) - dhy_z)
+        ey = income[3, layer, :] - d * dhz
+        ez = income[4, layer, :] + d * dhy
+        for i, f in enumerate((ex, ey, ez)):
+            e1[i, z, at, :] = edge_lanes(f, i, 0, z)
+        d = income[8, layer, :]
+        ey = income[6, layer, :] + d * h1[2, z + 1, 23:24, :]
+        ez = income[7, layer, :] - d * h1[1, z + 1, 23:24, :]
+        for i, f in enumerate((ey, ez)):
+            e1[i + 1, z, 24:25, :] = edge_lanes(f, i + 1, 1, z)
+
     def first_e(z, _):
-        for r in (7, 15, 23):
+        for r in (8, 16):
             rows = slice(r, r + 8)
             turn = main_curl(h1, z, r, sh1)
             d = ad[3, z, rows, :]
@@ -286,7 +349,13 @@
         return 0
 
     lax.fori_loop(0, NZ, first_e, 0, unroll=NZ)
-    main_h(e1, 0, h1, 0, se1, h2, (7, 15, 23))
+    main_h(e1, 0, h1, 0, se1, h2, (8, 16))
+    for z in range(NZ):
+        ex, ey, ez = (e1[i, z, at, :] for i in range(3))
+        ex_y = jnp.where(line == 127, pltpu.roll(se1[0, at, :], 125 - 8 * z, 1), pltpu.roll(ex, 127, 1))
+        h2[1, z + 1, at, :] = h1[1, z + 1, at, :] - DT * ((e1[0, z + 1, at, :] - ex) - (e1[2, z, 8:9, :] - ez))
+        h2[2, z + 1, at, :] = h1[2, z + 1, at, :] - DT * ((e1[1, z, 8:9, :] - ey) - (ex_y - ex))
+
     def second_e(z, _):
         for b in (0, 8):
             rows, here = slice(TOP + b, TOP + b + 8), slice(b, b + 8)
@@ -298,7 +367,7 @@
         return 0
 
     lax.fori_loop(0, NZ, second_e, 0, unroll=NZ)
-    for c in first + second:
+    for c in sends:
         c.wait_send()
 
 
@@ -346,9 +415,15 @@
             pltpu.VMEM((3, 40, LANES), f32),
             pltpu.VMEM((3, 40, LANES), f32),
             pltpu.VMEM((3, 40, LANES), f32),
-            pltpu.SemaphoreType.DMA((9,)),
-            pltpu.SemaphoreType.DMA((18,)),
-            pltpu.SemaphoreType.DMA((18,)),
+            pltpu.VMEM((4, 3, 32, LANES), f32),
+            pltpu.VMEM((3, 3, 32, LANES), f32),
+            pltpu.VMEM((2, 3, 32, LANES), f32),
+            pltpu.VMEM((9, NZ, LANES), f32),
+            pltpu.VMEM((9, NZ, LANES), f32),
+            pltpu.VMEM((3, 2, LANES), f32),
+            pltpu.SemaphoreType.DMA((16,)),
+            pltpu.SemaphoreType.DMA((11,)),
+            pltpu.SemaphoreType.DMA((11,)),
         ],
         compiler_params=pltpu.CompilerParams(
             collective_id=0, has_side_effects=True, vmem_limit_bytes=48 * 1024 * 1024

time: 23.9 us -> 22.4 us (0.937)
  the two profiles are of different devices: /device:TPU:8 before, /device:TPU:1 now
where the time goes in v4:
time: 22.4 us; the launch traced here: 22.3 us
  Pallas kernels  21.6 us (96%)
  between operations  0.64 us (3%)
    pallas_call x1, Pallas kernels, body(): pl.pallas_call(kernel, out_shape=(block, block), in_specs=[hbm] * 9, out_...  20.7 us
    pallas_call x1, Pallas kernels, body(): pl.pallas_call(write_out, out_shape=(pltpu.HBM(e_field.shape, f32),) * 2,...  0.89 us

profile of v4, /device:TPU:1, one launch (start us, length us, event | category | flops | bytes accessed | tf_op | source)
XLA Modules:
  0.0 22.3 jit_solution(5616153566537892620)
XLA Ops:
  0.6 20.7 %shard_map.104 = (f32[3,16,16,128]{3,2,1,0:T(8,128)S(1)}, f32[3,16,16,128]{3,2,1,0:T(8,128)S(1)}) custom-call(f32[3,16,16,128]{3,2,1,0:T(8,128)} %e_hbm.1, f32[3,16,16,128]{3,2,1,0:T(8,128)} %h_hbm.1, f32[2,3,16,16,128]{4,3,2,1,0:T(8,128)} %now_hbm.1, f32[2,3,16,16,128]{4,3,2,1,0:T(8,128)} %prev_hbm.1, s32[16,16,128]{2,1,0:T(8,128)} %mat_hbm.1, f32[4]{0:T(128)} %eps_hbm.1, ...), custom_call_target="tpu_custom_call" | custom-call | tf_op jit(solution)/shard_map/pallas_call | solution.py:392
  21.4 0.9 %shard_map.105 = (f32[3,16,16,128]{3,2,1,0:T(8,128)}, f32[3,16,16,128]{3,2,1,0:T(8,128)}) custom-call(f32[3,16,16,128]{3,2,1,0:T(8,128)S(1)} %get-tuple-element.4.e_ref, f32[3,16,16,128]{3,2,1,0:T(8,128)S(1)} %get-tuple-element.5.h_ref), custom_call_target="tpu_custom_call" | custom-call | tf_op jit(solution)/shard_map/pallas_call | solution.py:433

commit v5 on v4

--- a/solution.py
+++ b/solution.py
@@ -50,7 +50,7 @@
     e_out, h_out,
     eps_ref, res_ref, damp_ref, str_ref,
     eh, ad, now, prev, mat, tables, keep, late, h1, e1, h2,
-    strips, wide, sh1, se1, sh2, edge_e, edge_h, edge_new, outgo, income, ring,
+    strips, wide, sh1, se1, sh2, edge_e, edge_h, edge_new, outgo, income, fix,
     load_sem, send_sem, recv_sem,
 ):
     gx, gy = lax.axis_index("gx"), lax.axis_index("gy")
@@ -97,6 +97,7 @@
         h1[c, 0] = zero
         h2[c, 0] = zero
         for k in range(4):
+            edge_e[k, c, 0:8, :] = jnp.zeros(TILE, jnp.float32)
             edge_e[k, c, 24:32, :] = jnp.zeros(TILE, jnp.float32)
         for k in range(2):
             edge_new[k, c, 0:8, :] = jnp.zeros(TILE, jnp.float32)
@@ -155,7 +156,7 @@
                 late[c, z, b : b + 8, :] = (r * f + (p0 * n0 + p1 * n1)) + (q0 * m0 + q1 * m1)
         return 0
 
-    lax.fori_loop(0, NZ, local, 0, unroll=8)
+    lax.fori_loop(0, NZ, local, 0, unroll=NZ)
     pack(range(8, 12))
     for c in loads[9:]:
         c.wait()
@@ -207,6 +208,11 @@
     outgo[7] = ad[2, :, 8, :] + d * (hy - (hx - pltpu.roll(hx, 1, 1)))
     outgo[8] = d
 
+    fix[0] = DT * edge_e[0, 2, span, :]
+    dhz = -DT * edge_e[0, 1, span, :]
+    fix[1] = dhz
+    fix[2] = (dhz - pltpu.roll(dhz, 1, 1)) - (fix[0] - DT * edge_e[0, 2, down, :])
+
     a, b = pl.ds(22, 2), pl.ds(8, 2)
     low, high = pl.ds(6, 2), pl.ds(24, 2)
     mid = pl.ds(TOP, ROWS)
@@ -239,10 +245,6 @@
                     f = jnp.where(q < 4, jnp.where(q < 2, right, after), jnp.where(q < 6, before, left))
                     wide[i, rows, :] = pltpu.roll(f, LANES - p, 1) if p else f
 
-    for c in sends:
-        c.wait_recv()
-    widen(range(6), (6, 14, 22))
-    widen(range(8, 12), (7, 15, 23))
 
     def ahead_z(f):
         return jnp.where(lane < 120, pltpu.roll(f, 120, 1), 0.0)
@@ -293,6 +295,14 @@
             h_ref[0, z, rows, :], h_ref[1, z, rows, :],
         )
 
+    for c in (sends[4], sends[5], sends[8]):
+        c.wait_recv()
+    widen((0, 2), (8, 16))
+    main_h(eh, 1, eh, 3, wide, h1, (8, 16))
+    for c in sends[0:4] + sends[6:8] + sends[9:]:
+        c.wait_recv()
+    widen(range(6), (6, 14, 22))
+    widen(range(8, 12), (7, 15, 23))
     strip_h(wide, wide, 3, sh1, (6, 14, 22))
     for r in (7, 15, 23):
         rows, back_rows = slice(r, r + 8), slice(r - 1, r + 7)
@@ -306,38 +316,32 @@
             se1[i, rows, :] = wide[8 + i, rows, :] + d * turn[i]
     strip_h(se1, sh1, 0, sh2, (7, 15, 23))
 
-    line = lane[0:1, :]
-    for k, r in enumerate((7, 24)):
-        for i in range(3):
-            f = se1[i, r : r + 1, :]
-            ring[i, k : k + 1, :] = jnp.where((line & 7) == 2, pltpu.roll(f, 124, 1), f)
-
-    def edge_lanes(f, i, k, z):
-        wrapped = pltpu.roll(ring[i, k : k + 1, :], 126 - 8 * z, 1)
-        return jnp.where((line == 0) | (line == 127), wrapped, f)
-
-    main_h(eh, 1, eh, 3, wide, h1, (8, 16))
-    at = slice(7, 8)
-    for z in range(NZ):
-        layer = slice(z, z + 1)
-        dhy = DT * eh[2, z + 1, 8:9, :]
-        dhz = -DT * eh[1, z + 1, 8:9, :]
-        dhy_z = dhy if z == 0 else dhy - DT * eh[2, z, 8:9, :]
-        h1[1, z + 1, at, :] = income[0, layer, :] + dhy
-        h1[2, z + 1, at, :] = jnp.where(
-            line == 127, pltpu.roll(sh1[2, at, :], 126 - 8 * z, 1), income[1, layer, :] + dhz
-        )
-        d = income[5, layer, :]
-        ex = income[2, layer, :] + d * ((dhz - pltpu.roll(dhz, 1, 1)) - dhy_z)
-        ey = income[3, layer, :] - d * dhz
-        ez = income[4, layer, :] + d * dhy
-        for i, f in enumerate((ex, ey, ez)):
-            e1[i, z, at, :] = edge_lanes(f, i, 0, z)
-        d = income[8, layer, :]
-        ey = income[6, layer, :] + d * h1[2, z + 1, 23:24, :]
-        ez = income[7, layer, :] - d * h1[1, z + 1, 23:24, :]
-        for i, f in enumerate((ey, ez)):
-            e1[i + 1, z, 24:25, :] = edge_lanes(f, i + 1, 1, z)
+    column = lax.broadcasted_iota(jnp.int32, (NZ, LANES), 1)
+    start = 8 * lax.broadcasted_iota(jnp.int32, (NZ, LANES), 0)
+
+    def pick(f, q):
+        f = jnp.broadcast_to(f, (NZ, LANES))
+        return jnp.sum(jnp.where(column == start + q, f, 0.0), axis=1, keepdims=True)
+
+    def edge_lanes(f, i, row):
+        line = se1[i, row : row + 1, :]
+        return jnp.where(column == 127, pick(line, 1), jnp.where(column == 0, pick(line, 6), f))
+
+    at, layers, shifted = slice(7, 8), slice(0, NZ), slice(1, NZ + 1)
+    hy_row = income[0] + fix[0]
+    hz_row = jnp.where(column == 127, pick(sh1[2, at, :], 1), income[1] + fix[1])
+    d = income[5]
+    e_row = [
+        edge_lanes(f, i, 7)
+        for i, f in enumerate((income[2] + d * fix[2], income[3] - d * fix[1], income[4] + d * fix[0]))
+    ]
+    h1[1, shifted, 7, :] = hy_row
+    h1[2, shifted, 7, :] = hz_row
+    for i in range(3):
+        e1[i, layers, 7, :] = e_row[i]
+    d = income[8]
+    e1[1, layers, 24, :] = edge_lanes(income[6] + d * h1[2, shifted, 23, :], 1, 24)
+    e1[2, layers, 24, :] = edge_lanes(income[7] - d * h1[1, shifted, 23, :], 2, 24)
 
     def first_e(z, _):
         for r in (8, 16):
@@ -350,11 +354,10 @@
 
     lax.fori_loop(0, NZ, first_e, 0, unroll=NZ)
     main_h(e1, 0, h1, 0, se1, h2, (8, 16))
-    for z in range(NZ):
-        ex, ey, ez = (e1[i, z, at, :] for i in range(3))
-        ex_y = jnp.where(line == 127, pltpu.roll(se1[0, at, :], 125 - 8 * z, 1), pltpu.roll(ex, 127, 1))
-        h2[1, z + 1, at, :] = h1[1, z + 1, at, :] - DT * ((e1[0, z + 1, at, :] - ex) - (e1[2, z, 8:9, :] - ez))
-        h2[2, z + 1, at, :] = h1[2, z + 1, at, :] - DT * ((e1[1, z, 8:9, :] - ey) - (ex_y - ex))
+    ex, ey, ez = e_row
+    ex_y = jnp.where(column == 127, pick(se1[0, at, :], 2), pltpu.roll(ex, 127, 1))
+    h2[1, shifted, 7, :] = hy_row - DT * ((e1[0, shifted, 7, :] - ex) - (e1[2, layers, 8, :] - ez))
+    h2[2, shifted, 7, :] = hz_row - DT * ((e1[1, layers, 8, :] - ey) - (ex_y - ex))
 
     def second_e(z, _):
         for b in (0, 8):
@@ -420,7 +423,7 @@
             pltpu.VMEM((2, 3, 32, LANES), f32),
             pltpu.VMEM((9, NZ, LANES), f32),
             pltpu.VMEM((9, NZ, LANES), f32),
-            pltpu.VMEM((3, 2, LANES), f32),
+            pltpu.VMEM((3, NZ, LANES), f32),
             pltpu.SemaphoreType.DMA((16,)),
             pltpu.SemaphoreType.DMA((11,)),
             pltpu.SemaphoreType.DMA((11,)),

time: 22.4 us -> 22.2 us (level)
    pallas_call x1, Pallas kernels: 20.7 us -> 20.5 us  [body(): pl.pallas_call(kernel, out_shape=(block, block), in_specs=[hbm] * 9, out_...]
where the time goes in v5:
time: 22.2 us; the launch traced here: 22 us
  Pallas kernels  21.4 us (96%)
  between operations  0.64 us (3%)
    pallas_call x1, Pallas kernels, body(): pl.pallas_call(kernel, out_shape=(block, block), in_specs=[hbm] * 9, out_...  20.5 us
    pallas_call x1, Pallas kernels, body(): pl.pallas_call(write_out, out_shape=(pltpu.HBM(e_field.shape, f32),) * 2,...  0.89 us

profile of v5, /device:TPU:1, one launch (start us, length us, event | category | flops | bytes accessed | tf_op | source)
XLA Modules:
  0.0 22.0 jit_solution(6039177327524046519)
XLA Ops:
  0.6 20.5 %shard_map.104 = (f32[3,16,16,128]{3,2,1,0:T(8,128)S(1)}, f32[3,16,16,128]{3,2,1,0:T(8,128)S(1)}) custom-call(f32[3,16,16,128]{3,2,1,0:T(8,128)} %e_hbm.1, f32[3,16,16,128]{3,2,1,0:T(8,128)} %h_hbm.1, f32[2,3,16,16,128]{4,3,2,1,0:T(8,128)} %now_hbm.1, f32[2,3,16,16,128]{4,3,2,1,0:T(8,128)} %prev_hbm.1, s32[16,16,128]{2,1,0:T(8,128)} %mat_hbm.1, f32[4]{0:T(128)} %eps_hbm.1, ...), custom_call_target="tpu_custom_call" | custom-call | tf_op jit(solution)/shard_map/pallas_call | solution.py:395
  21.1 0.9 %shard_map.105 = (f32[3,16,16,128]{3,2,1,0:T(8,128)}, f32[3,16,16,128]{3,2,1,0:T(8,128)}) custom-call(f32[3,16,16,128]{3,2,1,0:T(8,128)S(1)} %get-tuple-element.4.e_ref, f32[3,16,16,128]{3,2,1,0:T(8,128)S(1)} %get-tuple-element.5.h_ref), custom_call_target="tpu_custom_call" | custom-call | tf_op jit(solution)/shard_map/pallas_call | solution.py:436

commit v6 on v5

--- a/solution.py
+++ b/solution.py
@@ -218,10 +218,10 @@
     mid = pl.ds(TOP, ROWS)
     pl.semaphore_wait(barrier, 8)
     sends = [
-        send(0, strips.at[0, :, a, :], strips.at[2, :, low, :], (xn, yn)),
+        send(0, strips.at[0, 0:2, a, :], strips.at[2, 0:2, low, :], (xn, yn)),
         send(1, strips.at[1, :, a, :], strips.at[3, :, low, :], (xn, yp)),
         send(2, strips.at[0, :, b, :], strips.at[2, :, high, :], (xp, yn)),
-        send(3, strips.at[1, :, b, :], strips.at[3, :, high, :], (xp, yp)),
+        send(3, strips.at[1, 0:2, b, :], strips.at[3, 0:2, high, :], (xp, yp)),
         send(4, strips.at[0, :, mid, :], strips.at[2, :, mid, :], (gx, yn)),
         send(5, strips.at[1, :, mid, :], strips.at[3, :, mid, :], (gx, yp)),
         send(6, strips.at[0:2, :, a, :], strips.at[0:2, :, low, :], (xn, gy)),

time: 22.2 us -> 22.2 us (level)
  no operation moved by 1% of the time
where the time goes in v6:
time: 22.2 us; the launch traced here: 22 us
  Pallas kernels  21.4 us (96%)
  between operations  0.64 us (3%)
    pallas_call x1, Pallas kernels, body(): pl.pallas_call(kernel, out_shape=(block, block), in_specs=[hbm] * 9, out_...  20.5 us
    pallas_call x1, Pallas kernels, body(): pl.pallas_call(write_out, out_shape=(pltpu.HBM(e_field.shape, f32),) * 2,...  0.89 us

profile of v6, /device:TPU:1, one launch (start us, length us, event | category | flops | bytes accessed | tf_op | source)
XLA Modules:
  0.0 22.0 jit_solution(4959184112073198797)
XLA Ops:
  0.6 20.5 %shard_map.104 = (f32[3,16,16,128]{3,2,1,0:T(8,128)S(1)}, f32[3,16,16,128]{3,2,1,0:T(8,128)S(1)}) custom-call(f32[3,16,16,128]{3,2,1,0:T(8,128)} %e_hbm.1, f32[3,16,16,128]{3,2,1,0:T(8,128)} %h_hbm.1, f32[2,3,16,16,128]{4,3,2,1,0:T(8,128)} %now_hbm.1, f32[2,3,16,16,128]{4,3,2,1,0:T(8,128)} %prev_hbm.1, s32[16,16,128]{2,1,0:T(8,128)} %mat_hbm.1, f32[4]{0:T(128)} %eps_hbm.1, ...), custom_call_target="tpu_custom_call" | custom-call | tf_op jit(solution)/shard_map/pallas_call | solution.py:395
  21.1 0.9 %shard_map.105 = (f32[3,16,16,128]{3,2,1,0:T(8,128)}, f32[3,16,16,128]{3,2,1,0:T(8,128)}) custom-call(f32[3,16,16,128]{3,2,1,0:T(8,128)S(1)} %get-tuple-element.4.e_ref, f32[3,16,16,128]{3,2,1,0:T(8,128)S(1)} %get-tuple-element.5.h_ref), custom_call_target="tpu_custom_call" | custom-call | tf_op jit(solution)/shard_map/pallas_call | solution.py:436
